TPU v7x, 32 devices: a whole 2x2x4 slice. The times are simulated.
32 devices in a mesh: replica: 2 (over x), outer: 4 (over y, core), link: 4 (over z).
Axes of the slice: x: 2, y: 2, z: 4, core: 2. Of those that a mesh axis runs over, the one named last changes fastest.
Arguments:
- link_in: bfloat16 [2, 8192, 256], P('replica', ('outer', 'link')), may hold values from -6 to 6
- path_in: bfloat16 [2, 2048, 256], P('replica', ('outer', 'link')), may hold values from -6 to 6
- hop_slots: int32 [2, 2048, 24], P('replica', ('outer', 'link')), may hold values from 0 to 1023
- hop_lens: int32 [2, 2048], P('replica', ('outer', 'link')), may hold values from 2 to 24
- failed: int32 [2, 8192], P('replica', ('outer', 'link')), may hold values 0 or 1
- serve_index: int32 [2, 16, 16, 64], P('replica', None, ('outer', 'link')), may hold values from 0 to 511
- link_grad: bfloat16 [2, 8192, 256], P('replica', ('outer', 'link')), may hold values from -6 to 6
- path_grad: bfloat16 [2, 2048, 256], P('replica', ('outer', 'link')), may hold values from -6 to 6
- gru_wx: bfloat16 [256, 768], replicated, may hold values from -0.375 to 0.375
- gru_wh: bfloat16 [256, 768], replicated, may hold values from -0.375 to 0.375
- gru_bias: float32 [768], replicated, may hold values from -3 to 3
- mlp_w1: bfloat16 [512, 256], replicated, may hold values from -0.25 to 0.25
- mlp_b1: float32 [256], replicated, may hold values from -3 to 3
- mlp_w2: bfloat16 [256, 256], replicated, may hold values from -0.375 to 0.375
- mlp_b2: float32 [256], replicated, may hold values from -3 to 3
Outputs:
- link_out: bfloat16 [2, 8192, 256], P('replica', ('outer', 'link'))
- path_out: bfloat16 [2, 2048, 256], P('replica', ('outer', 'link'))
- link_in_grad: float32 [2, 8192, 256], P('replica', ('outer', 'link'))
- path_in_grad: float32 [2, 2048, 256], P('replica', ('outer', 'link'))
- grad_wx: float32 [256, 768], replicated
- grad_wh: float32 [256, 768], replicated
- grad_bias: float32 [768], replicated
- grad_w1: float32 [512, 256], replicated
- grad_b1: float32 [256], replicated
- grad_w2: float32 [256, 256], replicated
- grad_b2: float32 [256], replicated
Inputs may be any that keep to these rules, and one draw needn't show every extreme that they name: `serve_index`: entry [s, d, o, c] names, among the 512 links of owner device o, the link in request slot c of device d; a link may fill several slots. `hop_slots`: slot o * 64 + c is request slot c of the flow's own device towards owner o; entries at hops past the flow's length are ignored. 1 marks a failed link.
All inputs are finite; a program needn't handle non-finite values. No bound on the sum of `failed` on one device may be relied on, other than what follows from the above.
Results may differ from a plain program's by a relative error of at most 0.0067.
Values may be sent and summed in bfloat16 or wider, within the bound.
A program may use at most 128 MiB of HBM per device.

v0:
```python
import jax
import jax.numpy as jnp
from jax import lax
from jax.sharding import PartitionSpec as P


def gate_terms(state_now, hop_input, input_weight, hidden_weight, gate_bias):
    from_input = jnp.dot(hop_input, input_weight, preferred_element_type=jnp.float32) + gate_bias
    from_state = jnp.dot(
        state_now.astype(jnp.bfloat16), hidden_weight, preferred_element_type=jnp.float32
    )
    return (from_input, from_state)


def gru_cell(state_now, from_input, from_state):
    feat_width = state_now.shape[1]
    update = jax.nn.sigmoid(from_input[:, :feat_width] + from_state[:, :feat_width])
    reset = jax.nn.sigmoid(
        from_input[:, feat_width : 2 * feat_width] + from_state[:, feat_width : 2 * feat_width]
    )
    candidate = jnp.tanh(from_input[:, 2 * feat_width :] + reset * from_state[:, 2 * feat_width :])
    return (candidate + update * (state_now - candidate), update, reset, candidate)


def gru_forward(path_start, hop_inputs, live_mask, input_weight, hidden_weight, gate_bias):

    def advance(state_now, scan_item):
        hop_input, live_now = scan_item
        from_input, from_state = gate_terms(
            state_now, hop_input, input_weight, hidden_weight, gate_bias
        )
        stepped = gru_cell(state_now, from_input, from_state)[0]
        state_next = jnp.where(live_now[:, None] > 0, stepped, state_now)
        return (state_next, (state_next,))

    return lax.scan(advance, path_start.astype(jnp.float32), (hop_inputs, live_mask))[1]


def back_step(
    carried, hop_input, state_now, live_now, hop_grad, from_input, from_state, input_tr, hidden_tr
):
    grad_state, grad_wx, grad_wh, grad_bias = carried
    feat_width = state_now.shape[1]
    live_col = live_now[:, None]
    grad_state = grad_state + live_col * hop_grad
    update, reset, candidate = gru_cell(state_now, from_input, from_state)[1:]
    pre_update = grad_state * (state_now - candidate) * update * (1.0 - update)
    pre_cand = grad_state * (1.0 - update) * (1.0 - candidate * candidate)
    pre_reset = pre_cand * from_state[:, 2 * feat_width :] * reset * (1.0 - reset)
    grad_in = jnp.concatenate([pre_update, pre_reset, pre_cand], axis=1) * live_col
    grad_hid = jnp.concatenate([pre_update, pre_reset, pre_cand * reset], axis=1) * live_col
    in_bf = grad_in.astype(jnp.bfloat16)
    hid_bf = grad_hid.astype(jnp.bfloat16)
    grad_prev = jnp.where(
        live_col > 0,
        grad_state * update + jnp.dot(hid_bf, hidden_tr, preferred_element_type=jnp.float32),
        grad_state,
    )
    grad_input = jnp.dot(in_bf, input_tr, preferred_element_type=jnp.float32)
    grad_wx = grad_wx + jnp.dot(hop_input.T, in_bf, preferred_element_type=jnp.float32)
    grad_wh = grad_wh + jnp.dot(
        state_now.astype(jnp.bfloat16).T, hid_bf, preferred_element_type=jnp.float32
    )
    grad_bias = grad_bias + jnp.sum(grad_in, axis=0)
    return ((grad_prev, grad_wx, grad_wh, grad_bias), grad_input)


def gru_backward(
    path_start,
    states,
    hop_inputs,
    live_mask,
    hop_grads,
    path_grad,
    input_weight,
    hidden_weight,
    gate_bias,
):
    feat_width = path_start.shape[1]
    prior_states = jnp.concatenate([path_start.astype(jnp.float32)[None], states[:-1]], axis=0)
    input_tr = input_weight.T
    hidden_tr = hidden_weight.T
    initial = (
        path_grad.astype(jnp.float32),
        jnp.zeros((feat_width, 3 * feat_width), jnp.float32),
        jnp.zeros((feat_width, 3 * feat_width), jnp.float32),
        jnp.zeros((3 * feat_width,), jnp.float32),
    )

    def retreat(carried, scan_item):
        hop_input, state_now, live_now, hop_grad = scan_item
        from_input, from_state = gate_terms(
            state_now, hop_input, input_weight, hidden_weight, gate_bias
        )
        return back_step(
            carried,
            hop_input,
            state_now,
            live_now,
            hop_grad,
            from_input,
            from_state,
            input_tr,
            hidden_tr,
        )

    scan_items = (hop_inputs, prior_states, live_mask, hop_grads)
    return lax.scan(retreat, initial, scan_items, reverse=True)


def link_forward(link_rows, agg_bf, keep_col, mlp_w1, mlp_b1, mlp_w2, mlp_b2):
    feat_width = link_rows.shape[1]
    pre_act = (
        jnp.dot(link_rows, mlp_w1[:feat_width], preferred_element_type=jnp.float32)
        + jnp.dot(agg_bf, mlp_w1[feat_width:], preferred_element_type=jnp.float32)
        + mlp_b1
    )
    activ = jax.nn.silu(pre_act).astype(jnp.bfloat16)
    value = (
        link_rows.astype(jnp.float32)
        + jnp.dot(activ, mlp_w2, preferred_element_type=jnp.float32)
        + mlp_b2
    )
    return ((keep_col * value).astype(jnp.bfloat16), pre_act, activ)


def link_backward(link_grad_rows, link_rows, agg_bf, keep_col, pre_act, activ, mlp_w1, mlp_w2):
    feat_width = link_rows.shape[1]
    grad_val = keep_col * link_grad_rows.astype(jnp.float32)
    val_bf = grad_val.astype(jnp.bfloat16)
    grad_w2 = jnp.dot(activ.T, val_bf, preferred_element_type=jnp.float32)
    grad_b2 = jnp.sum(grad_val, axis=0)
    grad_act = jnp.dot(val_bf, mlp_w2.T, preferred_element_type=jnp.float32)
    sigma = jax.nn.sigmoid(pre_act)
    grad_pre = grad_act * sigma * (1.0 + pre_act * (1.0 - sigma))
    pre_bf = grad_pre.astype(jnp.bfloat16)
    grad_w1 = jnp.concatenate(
        [
            jnp.dot(link_rows.T, pre_bf, preferred_element_type=jnp.float32),
            jnp.dot(agg_bf.T, pre_bf, preferred_element_type=jnp.float32),
        ],
        axis=0,
    )
    grad_b1 = jnp.sum(grad_pre, axis=0)
    link_direct = grad_val + jnp.dot(
        pre_bf, mlp_w1[:feat_width].T, preferred_element_type=jnp.float32
    )
    agg_grad = jnp.dot(pre_bf, mlp_w1[feat_width:].T, preferred_element_type=jnp.float32).astype(
        jnp.bfloat16
    )
    return (link_direct, agg_grad, (grad_w1, grad_b1, grad_w2, grad_b2))


def swap_slots(blocks):
    return lax.all_to_all(blocks, ("outer", "link"), split_axis=0, concat_axis=0, tiled=True)


def body(
    link_in,
    path_in,
    hop_slots,
    hop_lens,
    failed,
    serve_index,
    link_grad,
    path_grad,
    gru_wx,
    gru_wh,
    gru_bias,
    mlp_w1,
    mlp_b1,
    mlp_w2,
    mlp_b2,
):
    link_rows = link_in[0]
    feat_width = link_rows.shape[1]
    link_count = link_rows.shape[0]
    serve_rows = serve_index[0, :, 0, :]
    group_size, slot_cap = serve_rows.shape
    serve_flat = serve_rows.reshape(-1)
    slot_ids = hop_slots[0].T
    hop_count, flow_count = slot_ids.shape
    flat_slots = slot_ids.reshape(-1)
    live_mask = (jnp.arange(hop_count, dtype=jnp.int32)[:, None] < hop_lens[0][None, :]).astype(
        jnp.float32
    )
    fetched = swap_slots(jnp.take(link_rows, serve_rows, axis=0))
    hop_inputs = jnp.take(fetched.reshape(group_size * slot_cap, feat_width), slot_ids, axis=0)
    states = gru_forward(path_in[0], hop_inputs, live_mask, gru_wx, gru_wh, gru_bias)[0]
    partial_value = jax.ops.segment_sum(
        (states * live_mask[:, :, None]).reshape(hop_count * flow_count, feat_width),
        flat_slots,
        num_segments=group_size * slot_cap,
    ).astype(jnp.bfloat16)
    arrived = swap_slots(partial_value.reshape(group_size, slot_cap, feat_width))
    aggregate = jax.ops.segment_sum(
        arrived.reshape(group_size * slot_cap, feat_width).astype(jnp.float32),
        serve_flat,
        num_segments=link_count,
    )
    agg_bf = aggregate.astype(jnp.bfloat16)
    keep_col = (1 - failed[0]).astype(jnp.float32)[:, None]
    link_out, pre_act, activ = link_forward(
        link_rows, agg_bf, keep_col, mlp_w1, mlp_b1, mlp_w2, mlp_b2
    )
    path_out = states[-1].astype(jnp.bfloat16)
    link_direct, agg_grad, mlp_terms = link_backward(
        link_grad[0], link_rows, agg_bf, keep_col, pre_act, activ, mlp_w1, mlp_w2
    )
    returned = swap_slots(jnp.take(agg_grad, serve_rows, axis=0))
    hop_grads = (
        jnp.take(returned.reshape(group_size * slot_cap, feat_width), slot_ids, axis=0).astype(
            jnp.float32
        )
        * live_mask[:, :, None]
    )
    finished, grad_inputs = gru_backward(
        path_in[0], states, hop_inputs, live_mask, hop_grads, path_grad[0], gru_wx, gru_wh, gru_bias
    )
    dpart = jax.ops.segment_sum(
        grad_inputs.reshape(hop_count * flow_count, feat_width),
        flat_slots,
        num_segments=group_size * slot_cap,
    ).astype(jnp.bfloat16)
    owned = swap_slots(dpart.reshape(group_size, slot_cap, feat_width))
    link_back = link_direct + jax.ops.segment_sum(
        owned.reshape(group_size * slot_cap, feat_width).astype(jnp.float32),
        serve_flat,
        num_segments=link_count,
    )
    summed = lax.psum(
        (
            finished[1],
            finished[2],
            finished[3],
            mlp_terms[0],
            mlp_terms[1],
            mlp_terms[2],
            mlp_terms[3],
        ),
        ("replica", "outer", "link"),
    )
    device_count = lax.axis_size("replica") * lax.axis_size("outer") * lax.axis_size("link")
    grad_scale = float(device_count * link_count) ** (-0.5)
    return (
        link_out[None],
        path_out[None],
        link_back[None],
        finished[0][None],
        summed[0] * grad_scale,
        summed[1] * grad_scale,
        summed[2] * grad_scale,
        summed[3] * grad_scale,
        summed[4] * grad_scale,
        summed[5] * grad_scale,
        summed[6] * grad_scale,
    )


def solution(mesh):
    return jax.shard_map(
        body,
        mesh=mesh,
        in_specs=(
            P("replica", ("outer", "link"), None),
            P("replica", ("outer", "link"), None),
            P("replica", ("outer", "link"), None),
            P("replica", ("outer", "link")),
            P("replica", ("outer", "link")),
            P("replica", None, ("outer", "link"), None),
            P("replica", ("outer", "link"), None),
            P("replica", ("outer", "link"), None),
            P(),
            P(),
            P(),
            P(),
            P(),
            P(),
            P(),
        ),
        out_specs=(
            P("replica", ("outer", "link"), None),
            P("replica", ("outer", "link"), None),
            P("replica", ("outer", "link"), None),
            P("replica", ("outer", "link"), None),
            P(),
            P(),
            P(),
            P(),
            P(),
            P(),
            P(),
        ),
        check_vma=False,
    )
```

profile of v0, /device:TPU:0, one launch (start us, length us, event | category | flops | bytes accessed | tf_op | source)
XLA Modules:
  0.0 529.9 jit_solution(17723859770806152092)
XLA Ops:
  8.7 4.5 gather_fusion
  14.2 7.4 %all-to-all-start = ((bf16[16,64,256]{2,1,0:T(8,128)(2,1)}), bf16[16,64,256]{2,1,0:T(8,128)(2,1)S(1)}, u32[]{:S(2)}, u32[]{:S(2)}) async-start(bf16[16,64,256]{2,1,0:T(8,128)(2,1)} %broadcast_select_fusion.2), calls=%async_computation | async-start | bytes 1048576 | tf_op jit(solution)/shard_map/all_to_all | solution.py:155
  21.7 15.6 %all-to-all-done = bf16[16,64,256]{2,1,0:T(8,128)(2,1)S(1)} async-done(((bf16[16,64,256]{2,1,0:T(8,128)(2,1)}), bf16[16,64,256]{2,1,0:T(8,128)(2,1)S(1)}, u32[]{:S(2)}, u32[]{:S(2)}) %all-to-all-start) | async-done | bytes 524320 | tf_op jit(solution)/shard_map/all_to_all | solution.py:155
  37.3 11.1 %gather_fusion.1 = bf16[3072,256]{1,0:T(8,128)(2,1)S(1)} fusion(bf16[1024,256]{1,0:T(8,128)(2,1)S(1)} %bitcast.136, s32[3072]{0:T(1024)S(1)} %bitcast_clamp_fusion), kind=kCustom, calls=%fused_computation.1.clone | custom fusion | bytes 3158016 | tf_op jit(solution)/shard_map/jit(_take)/gather | solution.py:188
  51.9 49.7 %while.35 = (s32[]{:T(128)}, f32[128,256]{1,0:T(8,128)S(1)}, f32[24,128,256]{2,1,0:T(8,128)}, f32[24,128]{1,0:T(8,128)S(1)}, bf16[24,128,256]{2,1,0:T(8,128)(2,1...) while((s32[]{:T(128)}, f32[128,256]{1,0:T(8,128)S(1)}, ...), condition=%wide.region_1.4_spmd, body=%wide.region_0.3_spmd.sunk | while | flops 101253248 | bytes 2953073 | solution.py:36
  101.6 4.0 broadcast_multiply_fusion
  105.6 17.7 %scatter_custom_fusion = f32[1024,256]{1,0:T(8,128)S(1)} fusion(s32[3072]{0:T(1024)S(1)} %bitcast.153, f32[3072,256]{1,0:T(8,128)} %bitcast.142, f32[]{:T(128)} %constant.108.clone.1), kind=kCustom, calls=%fused_computation.108 | custom fusion | flops 786432 | bytes 1049088 | tf_op jit(solution)/shard_map/scatter-add | solution.py:190
  124.2 3.6 all-to-all-start.1
  134.8 3.8 slice.91
  138.6 4.8 all-to-all-done.1
  144.2 6.1 %scatter_custom_fusion.1 = f32[512,256]{1,0:T(8,128)S(1)} fusion(s32[1024]{0:T(1024)} %reshape.174, bf16[1024,256]{1,0:T(8,128)(2,1)} %bitcast.146, f32[]{:T(128)} %constant.108.clone.1), kind=kCustom, calls=%fused_computation.98 | custom fusion | flops 524288 | bytes 1049088 | tf_op jit(solution)/shard_map/scatter-add | solution.py:196
  154.9 5.0 gather_fusion.2
  161.9 3.6 all-to-all-start.2
  165.8 3.9 pad_maximum_fusion.1
  172.2 8.9 %all-to-all-done.2 = bf16[16,64,256]{2,1,0:T(8,128)(2,1)S(1)} async-done(((bf16[16,64,256]{2,1,0:T(8,128)(2,1)}), bf16[16,64,256]{2,1,0:T(8,128)(2,1)S(1)}, u32[]{:S(2)}, u32[]{:S(2)}) %all-to-all-start.2) | async-done | bytes 524320 | tf_op jit(solution)/shard_map/all_to_all | solution.py:155
  181.1 12.9 %gather_fusion.3 = bf16[3072,256]{1,0:T(8,128)(2,1)} fusion(bf16[1024,256]{1,0:T(8,128)(2,1)S(1)} %bitcast.135, s32[3072]{0:T(1024)S(1)} %copy-done.27), kind=kCustom, calls=%fused_computation.3.clone | custom fusion | bytes 3158016 | tf_op jit(solution)/shard_map/jit(_take)/gather | solution.py:212
  194.1 4.1 convert_multiply_fusion
  200.2 176.4 %while.36 = (s32[]{:T(128)}, f32[128,256]{1,0:T(8,128)S(1)}, f32[256,768]{1,0:T(8,128)S(1)}, f32[256,768]{1,0:T(8,128)S(1)}, f32[768]{0:T(1024)S(1)}, /*index=5*...) while((s32[]{:T(128)}, f32[128,256]{1,0:T(8,128)S(1)}, ...), condition=%wide.region_6.9_spmd.clone, body=%wide.region_4.8_spmd.clone.sunk | while | flops 306152320 | bytes 14568985 | solution.py:108
  379.5 17.7 %scatter_custom_fusion.2 = f32[1024,256]{1,0:T(8,128)S(1)} fusion(s32[3072]{0:T(1024)} %bitcast.152, f32[3072,256]{1,0:T(8,128)} %bitcast.141, f32[]{:T(128)} %constant.108.clone.1), kind=kCustom, calls=%fused_computation.106 | custom fusion | flops 786432 | bytes 1049088 | tf_op jit(solution)/shard_map/scatter-add | solution.py:220
  398.1 3.6 all-to-all-start.3
  404.0 41.4 %all-reduce = (f32[768]{0:T(1024)S(1)}, f32[256]{0:T(256)S(1)}, f32[256]{0:T(256)S(1)}) all-reduce(f32[768]{0:T(1024)S(1)} %get-tuple-element.357, f32[256]{0:T(256)S(1)} %copy-done.35, f32[256]{0:T(256)S(1)} %fusion.60), channel_id=1, replica_groups=mesh['replica'=2,'outer'=4,'link'=4] {'replica','outer','link'}, use_global_device_ids=true, to_apply=%region_11.14 | all-reduce | flops 1280 | bytes 10240 | tf_op jit(solution)/shard_map/psum | solution.py:231
  447.1 6.5 %scatter_custom_fusion.3 = f32[512,256]{1,0:T(8,128)S(1)} fusion(f32[512,256]{1,0:T(8,128)S(1)} %convolution_add_fusion.5, s32[1024]{0:T(1024)} %reshape.174, bf16[1024,256]{1,0:T(8,128)(2,1)S(1)} %bitcast.145), kind=kCustom, calls=%fused_computation.96 | custom fusion | flops 524288 | bytes 1048576 | tf_op jit(solution)/shard_map/scatter-add | solution.py:226
  453.6 62.8 %all-reduce.4.cloned.1.call-done = (f32[256,768]{1,0:T(8,128)}, f32[256,768]{1,0:T(8,128)}, f32[512,256]{1,0:T(8,128)}, f32[256,256]{1,0:T(8,128)}) async-done(((f32[256,768]{1,0:T(8,128)}, f32[256,768]{1,0:T(8,128)}, f32[512,256]{1,0:T(8,128)}, f32[256,256]{1,0:T(8,128)}), (f32[256,768]{1,0:T(8,128)}, f32[256,768]{1,0:T(8,128)}, f32[512,256]{1,0:T(8,128)}, ...) | async-done | bytes 2359312 | tf_op jit(solution)/shard_map/psum | solution.py:231
  516.4 2.1 broadcast_multiply_fusion.2
  (597 shorter events, 261.8 us)
Async XLA Ops:
  7.2 144.7 %copy-start = (bf16[256,256]{1,0:T(8,128)(2,1)S(1)}, bf16[256,256]{1,0:T(8,128)(2,1)}, u32[]{:S(2)}) copy-start(bf16[256,256]{1,0:T(8,128)(2,1)} %param.36) | copy-start | bytes 393220
  7.9 6.3 %copy-start.31 = (pred[16,64]{1,0:T(8,128)(4,1)}, pred[16,64]{1,0:T(8,128)(4,1)S(1)}, u32[]{:S(2)}) copy-start(pred[16,64]{1,0:T(8,128)(4,1)S(1)} %compare_and_fusion.1) | copy-start | bytes 3076
  8.7 12.9 %copy-start.30 = (s32[1,128,24]{1,2,0:T(8,128)S(1)}, s32[1,128,24]{1,2,0:T(8,128)}, u32[]{:S(2)}) copy-start(s32[1,128,24]{1,2,0:T(8,128)} %param.25) | copy-start | bytes 36868
  8.7 12.9 %copy-start.36 = (s32[1,128]{1,0:T(1,128)S(1)}, s32[1,128]{1,0:T(1,128)}, u32[]{:S(2)}) copy-start(s32[1,128]{1,0:T(1,128)} %param.26) | copy-start | bytes 1540
  8.7 13.0 %copy-start.29 = (bf16[1,128,256]{2,1,0:T(8,128)(2,1)S(1)}, bf16[1,128,256]{2,1,0:T(8,128)(2,1)}, u32[]{:S(2)}) copy-start(bf16[1,128,256]{2,1,0:T(8,128)(2,1)} %param.24) | copy-start | bytes 196612
  14.2 23.1 %all-to-all-start = ((bf16[16,64,256]{2,1,0:T(8,128)(2,1)}), bf16[16,64,256]{2,1,0:T(8,128)(2,1)S(1)}, u32[]{:S(2)}, u32[]{:S(2)}) async-start(bf16[16,64,256]{2,1,0:T(8,128)(2,1)} %broadcast_select_fusion.2), calls=%async_computation | async-start | bytes 1048576 | tf_op jit(solution)/shard_map/all_to_all | solution.py:155
  21.6 26.7 %copy-start.26 = (s32[3072]{0:T(1024)}, s32[3072]{0:T(1024)S(1)}, u32[]{:S(2)}) copy-start(s32[3072]{0:T(1024)S(1)} %bitcast_clamp_fusion) | copy-start | bytes 36868
  105.6 24.5 %copy-start.28 = (s32[1,16,1,64]{3,2,1,0:T(1,128)S(1)}, s32[1,16,1,64]{3,2,1,0:T(1,128)}, u32[]{:S(2)}) copy-start(s32[1,16,1,64]{3,2,1,0:T(1,128)} %param.28) | copy-start | bytes 12292
  105.6 25.9 %copy-start.34 = (s32[1,512]{1,0:T(1,128)S(1)}, s32[1,512]{1,0:T(1,128)}, u32[]{:S(2)}) copy-start(s32[1,512]{1,0:T(1,128)} %param.27) | copy-start | bytes 6148
  105.6 27.3 %copy-start.1 = (bf16[1,512,256]{2,1,0:T(8,128)(2,1)S(1)}, bf16[1,512,256]{2,1,0:T(8,128)(2,1)}, u32[]{:S(2)}) copy-start(bf16[1,512,256]{2,1,0:T(8,128)(2,1)} %param.23) | copy-start | bytes 786436
  124.2 19.2 %all-to-all-start.1 = ((bf16[16,64,256]{2,1,0:T(8,128)(2,1)}), bf16[16,64,256]{2,1,0:T(8,128)(2,1)S(1)}, u32[]{:S(2)}, u32[]{:S(2)}) async-start(bf16[16,64,256]{2,1,0:T(8,128)(2,1)} %bitcast.17), calls=%async_computation.1 | async-start | bytes 1048576 | tf_op jit(solution)/shard_map/all_to_all | solution.py:155
  161.9 19.2 %all-to-all-start.2 = ((bf16[16,64,256]{2,1,0:T(8,128)(2,1)}), bf16[16,64,256]{2,1,0:T(8,128)(2,1)S(1)}, u32[]{:S(2)}, u32[]{:S(2)}) async-start(bf16[16,64,256]{2,1,0:T(8,128)(2,1)} %broadcast_select_fusion.1), calls=%async_computation.2 | async-start | bytes 1048576 | tf_op jit(solution)/shard_map/all_to_all | solution.py:155
  165.5 350.9 %all-reduce.4.cloned.1.call-start = ((), (), s32[]{:S(2)}) async-start(), calls=%async_computation.4 | async-start | bytes 4718592 | tf_op jit(solution)/shard_map/psum | solution.py:231
  169.7 11.4 %copy-start.27 = (s32[3072]{0:T(1024)S(1)}, s32[3072]{0:T(1024)}, u32[]{:S(2)}) copy-start(s32[3072]{0:T(1024)} %copy-done.26) | copy-start | bytes 36868
  181.1 12.9 %copy-start.25 = (f32[24,128]{1,0:T(8,128)S(1)}, f32[24,128]{1,0:T(8,128)}, u32[]{:S(2)}) copy-start(f32[24,128]{1,0:T(8,128)} %copy-done.24) | copy-start | bytes 36868
  200.2 177.6 %copy-start.16 = (bf16[1,512,256]{2,1,0:T(8,128)(2,1)S(1)}, bf16[1,512,256]{2,1,0:T(8,128)(2,1)}, u32[]{:S(2)}) copy-start(bf16[1,512,256]{2,1,0:T(8,128)(2,1)} %param.29) | copy-start | bytes 786436
  376.6 21.5 %copy-start.8 = (f32[128,256]{1,0:T(8,128)}, f32[128,256]{1,0:T(8,128)S(1)}, u32[]{:S(2)}) copy-start(f32[128,256]{1,0:T(8,128)S(1)} %get-tuple-element.354) | copy-start | bytes 393220
  376.6 25.0 %copy-start.37 = (f32[256]{0:T(256)S(1)}, f32[256]{0:T(256)}, u32[]{:S(2)}) copy-start(f32[256]{0:T(256)} %param.37) | copy-start | bytes 3076
  379.5 24.2 %copy-start.11 = (bf16[512,256]{1,0:T(8,128)(2,1)S(1)}, bf16[512,256]{1,0:T(8,128)(2,1)}, u32[]{:S(2)}) copy-start(bf16[512,256]{1,0:T(8,128)(2,1)} %copy-done.9) | copy-start | bytes 786436
  379.5 24.2 %copy-start.14 = (bf16[512,256]{1,0:T(8,128)(2,1)S(1)}, bf16[512,256]{1,0:T(8,128)(2,1)}, u32[]{:S(2)}) copy-start(bf16[512,256]{1,0:T(8,128)(2,1)} %param.34) | copy-start | bytes 786436
  397.2 6.8 %copy-start.35 = (f32[256]{0:T(256)S(1)}, f32[256]{0:T(256)}, u32[]{:S(2)}) copy-start(f32[256]{0:T(256)} %get-tuple-element.468) | copy-start | bytes 3076
  398.1 49.0 %all-to-all-start.3 = ((bf16[16,64,256]{2,1,0:T(8,128)(2,1)}), bf16[16,64,256]{2,1,0:T(8,128)(2,1)S(1)}, u32[]{:S(2)}, u32[]{:S(2)}) async-start(bf16[16,64,256]{2,1,0:T(8,128)(2,1)} %bitcast.30), calls=%async_computation.3 | async-start | bytes 1048576 | tf_op jit(solution)/shard_map/all_to_all | solution.py:155
  453.6 69.5 %copy-start.20 = (f32[512,256]{1,0:T(8,128)}, f32[512,256]{1,0:T(8,128)S(1)}, u32[]{:S(2)}) copy-start(f32[512,256]{1,0:T(8,128)S(1)} %scatter_custom_fusion.3) | copy-start | bytes 1572868
  516.4 5.7 %copy-start.17 = (f32[256,768]{1,0:T(8,128)S(1)}, f32[256,768]{1,0:T(8,128)}, u32[]{:S(2)}) copy-start(f32[256,768]{1,0:T(8,128)} %get-tuple-element.456) | copy-start | bytes 2359300
  (65 other events, 212.0 us)
Sparse Core Ops, SparseCore 0:
  377.9 138.4 all-reduce.3
where the time goes:
time: 536 us; the launch traced here: 530 us
  matrix products  182 us (34%)
  other arithmetic  130 us (24%)
  waiting for transfers between devices  92.1 us (17%)
  local copies, waits for them, and re-layouts  48.9 us (9%)
  blocking collectives  41.4 us (8%)
  starting transfers between devices  18.3 us (3%)
  between operations  14.4 us (3%)
    psum x1, waiting for transfers between devices, body(): lax.psum((finished[1], finished[2], finished[3], mlp_terms[0], mlp_terms[...  62.8 us
    dot_general x48, matrix products, gate_terms(): jnp.dot(hop_input, input_weight, preferred_element_type=jnp.float32)  50.9 us
    psum x1, blocking collectives, body(): lax.psum((finished[1], finished[2], finished[3], mlp_terms[0], mlp_terms[...  41.4 us
    dot_general x48, matrix products, gate_terms(): jnp.dot(state_now.astype(jnp.bfloat16), hidden_weight, preferred_element_...  33.1 us
    dot_general x24, matrix products, back_step(): jnp.dot(state_now.astype(jnp.bfloat16).T, hid_bf, preferred_element_type=...  31 us
    dot_general x24, matrix products, back_step(): jnp.dot(hop_input.T, in_bf, preferred_element_type=jnp.float32)  29.4 us
    all_to_all x4, waiting for transfers between devices, swap_slots(): lax.all_to_all(blocks, ('outer', 'link'), split_axis=0, concat_axis=0, ti...  29.3 us
    mul x24, other arithmetic, back_step(): pre_update = grad_state * (state_now - candidate) * update * (1.0 - update)  26.4 us
  transfers between devices with their start and end apart: 5, of which 4 were waited for; matrix products, arithmetic and copies ran while one was open for 9% of the time, Pallas kernels for 0%

commit v1 on v0

v1 whole, which is shorter than its diff:
```python
import functools

import jax
import jax.numpy as jnp
from jax import lax
from jax.experimental import pallas as pl
from jax.experimental.pallas import tpu as pltpu
from jax.sharding import PartitionSpec as P

VMEM_BYTES = 56 * 1024 * 1024


def mm(a, b):
    return jnp.dot(a, b, preferred_element_type=jnp.float32)


def mm_nt(a, b):
    return lax.dot_general(a, b, (((1,), (1,)), ((), ())), preferred_element_type=jnp.float32)


def mm_tn(a, b):
    return lax.dot_general(a, b, (((0,), (0,)), ((), ())), preferred_element_type=jnp.float32)


def sigmoid(v):
    return 0.5 * jnp.tanh(0.5 * v) + 0.5


def one_hot_rows(col, width):
    ids = lax.broadcasted_iota(jnp.int32, (col.shape[0], width), 1)
    return jnp.where(ids == col, 1.0, 0.0).astype(jnp.bfloat16)


def one_hot_cols(row, height):
    ids = lax.broadcasted_iota(jnp.int32, (height, row.shape[1]), 0)
    return jnp.where(ids == row, 1.0, 0.0).astype(jnp.bfloat16)


def whole(memory_space=pltpu.VMEM):
    return pl.BlockSpec(memory_space=memory_space)


def serve_kernel(col_ref, link_ref, out_ref):
    hot = one_hot_rows(col_ref[...], link_ref.shape[0])
    out_ref[...] = mm(hot, link_ref[...]).astype(jnp.bfloat16)


def forward_kernel(
    steps,
    fetched_ref,
    path_ref,
    col_ref,
    row_ref,
    lens_ref,
    wx_ref,
    wh_ref,
    bias_ref,
    xs_ref,
    hs_ref,
    coef_ref,
    partial_ref,
    path_out_ref,
    state,
    total,
    from_input,
    reached,
):
    block = pl.program_id(0)
    flows, width = path_ref.shape
    slots = fetched_ref.shape[0]

    @pl.when(block == 0)
    def _():
        state[...] = path_ref[...].astype(jnp.float32)
        total[...] = jnp.zeros_like(total)

    x = mm(one_hot_rows(col_ref[...], slots), fetched_ref[...]).astype(jnp.bfloat16)
    xs_ref[...] = x
    from_input[...] = mm(x, wx_ref[...]) + bias_ref[...]
    h = state[...]
    for u in range(steps):
        rows = pl.ds(u * flows, flows)
        live = lens_ref[...] > block * steps + u
        h_bf = h.astype(jnp.bfloat16)
        hs_ref[rows, :] = h_bf
        gs = mm(h_bf, wh_ref[...])
        gi = from_input[rows, :]
        z = sigmoid(gi[:, :width] + gs[:, :width])
        r = sigmoid(gi[:, width : 2 * width] + gs[:, width : 2 * width])
        gs3 = gs[:, 2 * width :]
        n = jnp.tanh(gi[:, 2 * width :] + r * gs3)
        diff = h - n
        h = jnp.where(live, n + z * diff, h)
        reached[rows, :] = jnp.where(live, h, 0.0).astype(jnp.bfloat16)
        rest = 1.0 - z
        c_n = jnp.where(live, rest * (1.0 - n * n), 0.0)
        coef_ref[rows, :width] = jnp.where(live, diff * z * rest, 0.0)
        coef_ref[rows, width : 2 * width] = c_n * gs3 * r * (1.0 - r)
        coef_ref[rows, 2 * width : 3 * width] = c_n
        coef_ref[rows, 3 * width : 4 * width] = c_n * r
        coef_ref[rows, 4 * width :] = jnp.where(live, z, 1.0)
    state[...] = h
    total[...] += mm(one_hot_cols(row_ref[0], slots), reached[...])

    @pl.when(block == pl.num_programs(0) - 1)
    def _():
        partial_ref[...] = total[...].astype(jnp.bfloat16)
        path_out_ref[...] = state[...].astype(jnp.bfloat16)


def link_kernel(
    arrived_ref,
    row_ref,
    col_ref,
    link_ref,
    grad_ref,
    keep_ref,
    w1_ref,
    b1_ref,
    w2_ref,
    b2_ref,
    link_out_ref,
    direct_ref,
    back_ref,
    grad_w_ref,
    grad_b_ref,
):
    links, width = link_ref.shape
    rows = link_ref[...]
    keep = keep_ref[...]
    agg = mm(one_hot_cols(row_ref[...], links), arrived_ref[...]).astype(jnp.bfloat16)
    u = mm(rows, w1_ref[:width, :]) + mm(agg, w1_ref[width:, :]) + b1_ref[...]
    s = sigmoid(u)
    act = (u * s).astype(jnp.bfloat16)
    value = rows.astype(jnp.float32) + mm(act, w2_ref[...]) + b2_ref[...]
    link_out_ref[...] = (keep * value).astype(jnp.bfloat16)
    gv = keep * grad_ref[...].astype(jnp.float32)
    gv_bf = gv.astype(jnp.bfloat16)
    du = mm_nt(gv_bf, w2_ref[...]) * s * (1.0 + u * (1.0 - s))
    du_bf = du.astype(jnp.bfloat16)
    d_agg = mm_nt(du_bf, w1_ref[width:, :]).astype(jnp.bfloat16)
    back_ref[...] = mm(one_hot_rows(col_ref[...], links), d_agg).astype(jnp.bfloat16)
    direct_ref[...] = gv + mm_nt(du_bf, w1_ref[:width, :])
    grad_w_ref[:width, :] = mm_tn(rows, du_bf)
    grad_w_ref[width : 2 * width, :] = mm_tn(agg, du_bf)
    grad_w_ref[2 * width :, :] = mm_tn(act, gv_bf)
    grad_b_ref[0:1, :] = jnp.sum(du, axis=0, keepdims=True)
    grad_b_ref[1:2, :] = jnp.sum(gv, axis=0, keepdims=True)


def backward_kernel(
    steps,
    returned_ref,
    path_grad_ref,
    col_ref,
    row_ref,
    lens_ref,
    wx_ref,
    wh_ref,
    xs_ref,
    hs_ref,
    coef_ref,
    dpart_ref,
    path_back_ref,
    grad_wx_ref,
    grad_wh_ref,
    grad_b_ref,
    carry,
    total,
    hop_grad,
    dgi,
    dgs,
    acc_wx,
    acc_wh,
    acc_b,
):
    block = pl.num_programs(0) - 1 - pl.program_id(0)
    flows, width = path_grad_ref.shape
    slots = returned_ref.shape[0]

    @pl.when(pl.program_id(0) == 0)
    def _():
        carry[...] = path_grad_ref[...].astype(jnp.float32)
        total[...] = jnp.zeros_like(total)
        acc_wx[...] = jnp.zeros_like(acc_wx)
        acc_wh[...] = jnp.zeros_like(acc_wh)
        acc_b[...] = jnp.zeros_like(acc_b)

    hop_grad[...] = mm(one_hot_rows(col_ref[...], slots), returned_ref[...])
    g = carry[...]
    for u in reversed(range(steps)):
        rows = pl.ds(u * flows, flows)
        live = lens_ref[...] > block * steps + u
        g = g + jnp.where(live, hop_grad[rows, :], 0.0)
        a_z = g * coef_ref[rows, :width]
        a_r = g * coef_ref[rows, width : 2 * width]
        a_n = g * coef_ref[rows, 2 * width : 3 * width]
        a_h = g * coef_ref[rows, 3 * width : 4 * width]
        z_bf = a_z.astype(jnp.bfloat16)
        r_bf = a_r.astype(jnp.bfloat16)
        dgs[rows, :width] = z_bf
        dgs[rows, width : 2 * width] = r_bf
        dgs[rows, 2 * width :] = a_h.astype(jnp.bfloat16)
        g = g * coef_ref[rows, 4 * width :] + mm_nt(dgs[rows, :], wh_ref[...])
        dgi[rows, :width] = z_bf
        dgi[rows, width : 2 * width] = r_bf
        dgi[rows, 2 * width :] = a_n.astype(jnp.bfloat16)
        for k, a in enumerate((a_z, a_r, a_n)):
            folded = jnp.sum(a.reshape(flows // 8, 8, width), axis=0)
            acc_b[:, k * width : (k + 1) * width] += folded
    carry[...] = g
    dx = mm_nt(dgi[...], wx_ref[...]).astype(jnp.bfloat16)
    total[...] += mm(one_hot_cols(row_ref[0], slots), dx)
    acc_wx[...] += mm_tn(xs_ref[...], dgi[...])
    acc_wh[...] += mm_tn(hs_ref[...], dgs[...])

    @pl.when(pl.program_id(0) == pl.num_programs(0) - 1)
    def _():
        dpart_ref[...] = total[...].astype(jnp.bfloat16)
        path_back_ref[...] = carry[...]
        emit_grads(acc_wx, acc_wh, acc_b, grad_wx_ref, grad_wh_ref, grad_b_ref)


def collect_kernel(owned_ref, row_ref, direct_ref, out_ref):
    hot = one_hot_cols(row_ref[...], direct_ref.shape[0])
    out_ref[...] = direct_ref[...] + mm(hot, owned_ref[...])


def call(kernel, out_shapes, **options):
    return pl.pallas_call(
        kernel,
        out_shape=[jax.ShapeDtypeStruct(shape, dtype) for shape, dtype in out_shapes],
        compiler_params=pltpu.CompilerParams(vmem_limit_bytes=VMEM_BYTES),
        **options,
    )


def emit_grads(acc_wx, acc_wh, acc_b, grad_wx_ref, grad_wh_ref, grad_b_ref):
    grad_wx_ref[...] = acc_wx[...]
    grad_wh_ref[...] = acc_wh[...]
    grad_b_ref[...] = jnp.sum(acc_b[...], axis=0, keepdims=True)


def swap_slots(rows, group, cap):
    blocks = rows.reshape(group, cap, rows.shape[1])
    moved = lax.all_to_all(blocks, ("outer", "link"), split_axis=0, concat_axis=0, tiled=True)
    return moved.reshape(group * cap, rows.shape[1])


def body(
    link_in,
    path_in,
    hop_slots,
    hop_lens,
    failed,
    serve_index,
    link_grad,
    path_grad,
    gru_wx,
    gru_wh,
    gru_bias,
    mlp_w1,
    mlp_b1,
    mlp_w2,
    mlp_b2,
):
    bf, f32 = jnp.bfloat16, jnp.float32
    link_rows = link_in[0]
    links, width = link_rows.shape
    serve_rows = serve_index[0, :, 0, :]
    group, cap = serve_rows.shape
    slots = group * cap
    serve_row = serve_rows.reshape(1, slots)
    serve_col = serve_rows.reshape(slots, 1)
    flows, hops = hop_slots.shape[1:]
    steps = 4 if hops % 4 == 0 else 1
    blocks = hops // steps
    slot_ids = hop_slots[0].T
    slot_col = slot_ids.reshape(hops * flows, 1)
    slot_row = slot_ids.reshape(blocks, 1, steps * flows)
    lens_col = hop_lens[0].reshape(flows, 1)
    keep_col = (1 - failed[0]).astype(f32)[:, None]
    span = steps * flows

    served = call(
        serve_kernel, [((slots, width), bf)], in_specs=[whole()] * 2, out_specs=[whole()]
    )(serve_col, link_rows)[0]
    fetched = swap_slots(served, group, cap)

    def fixed(*shape):
        return pl.BlockSpec(shape, lambda i: (0,) * len(shape))

    def ahead(*shape):
        return pl.BlockSpec(shape, lambda i: (i,) + (0,) * (len(shape) - 1))

    def behind(*shape):
        return pl.BlockSpec(shape, lambda i: (blocks - 1 - i,) + (0,) * (len(shape) - 1))

    xs, hs, coef, partial_value, path_out = call(
        functools.partial(forward_kernel, steps),
        [
            ((hops * flows, width), bf),
            ((hops * flows, width), bf),
            ((hops * flows, 5 * width), f32),
            ((slots, width), bf),
            ((flows, width), bf),
        ],
        grid=(blocks,),
        in_specs=[
            fixed(slots, width),
            fixed(flows, width),
            ahead(span, 1),
            ahead(1, 1, span),
            fixed(flows, 1),
            fixed(width, 3 * width),
            fixed(width, 3 * width),
            fixed(1, 3 * width),
        ],
        out_specs=[
            ahead(span, width),
            ahead(span, width),
            ahead(span, 5 * width),
            fixed(slots, width),
            fixed(flows, width),
        ],
        scratch_shapes=[
            pltpu.VMEM((flows, width), f32),
            pltpu.VMEM((slots, width), f32),
            pltpu.VMEM((span, 3 * width), f32),
            pltpu.VMEM((span, width), bf),
        ],
    )(fetched, path_in[0], slot_col, slot_row, lens_col, gru_wx, gru_wh, gru_bias[None])
    arrived = swap_slots(partial_value, group, cap)

    link_out, direct, back, grad_w, grad_b = call(
        link_kernel,
        [
            ((links, width), bf),
            ((links, width), f32),
            ((slots, width), bf),
            ((3 * width, width), f32),
            ((2, width), f32),
        ],
        in_specs=[whole()] * 10,
        out_specs=[whole()] * 5,
    )(
        arrived,
        serve_row,
        serve_col,
        link_rows,
        link_grad[0],
        keep_col,
        mlp_w1,
        mlp_b1[None],
        mlp_w2,
        mlp_b2[None],
    )
    returned = swap_slots(back, group, cap)

    dpart, path_back, grad_wx, grad_wh, grad_bias = call(
        functools.partial(backward_kernel, steps),
        grad_shapes(slots, flows, width),
        grid=(blocks,),
        in_specs=[
            fixed(slots, width),
            fixed(flows, width),
            behind(span, 1),
            behind(1, 1, span),
            fixed(flows, 1),
            fixed(width, 3 * width),
            fixed(width, 3 * width),
            behind(span, width),
            behind(span, width),
            behind(span, 5 * width),
        ],
        out_specs=[fixed(*shape) for shape, _ in grad_shapes(slots, flows, width)],
        scratch_shapes=[
            pltpu.VMEM((flows, width), f32),
            pltpu.VMEM((slots, width), f32),
            pltpu.VMEM((span, width), f32),
            pltpu.VMEM((span, 3 * width), bf),
            pltpu.VMEM((span, 3 * width), bf),
            pltpu.VMEM((width, 3 * width), f32),
            pltpu.VMEM((width, 3 * width), f32),
            pltpu.VMEM((8, 3 * width), f32),
        ],
    )(
        returned,
        path_grad[0],
        slot_col,
        slot_row,
        lens_col,
        gru_wx,
        gru_wh,
        xs,
        hs,
        coef,
    )
    everywhere = ("replica", "outer", "link")
    devices = lax.axis_size("replica") * lax.axis_size("outer") * lax.axis_size("link")
    scale = float(devices * links) ** (-0.5)
    owned, total_wx, total_wh, total_b, total_w, total_wb = finish(
        dpart, grad_wx, grad_wh, grad_bias, grad_w, grad_b, group, cap, scale, everywhere
    )
    link_back = call(
        collect_kernel, [((links, width), f32)], in_specs=[whole()] * 3, out_specs=[whole()]
    )(owned, serve_row, direct)[0]
    return (
        link_out[None],
        path_out[None],
        link_back[None],
        path_back[None],
        total_wx,
        total_wh,
        total_b,
        total_w[: 2 * width],
        total_wb[0],
        total_w[2 * width :],
        total_wb[1],
    )


def grad_shapes(slots, flows, width):
    return [
        ((slots, width), jnp.bfloat16),
        ((flows, width), jnp.float32),
        ((width, 3 * width), jnp.float32),
        ((width, 3 * width), jnp.float32),
        ((1, 3 * width), jnp.float32),
    ]


def finish(
    dpart, grad_wx, grad_wh, grad_bias, grad_w, grad_b, group, cap, scale, everywhere
):
    total_w, total_wb = lax.psum((grad_w, grad_b), everywhere)
    owned = swap_slots(dpart, group, cap)
    total_wx, total_wh, total_b = lax.psum((grad_wx, grad_wh, grad_bias[0]), everywhere)
    return (
        owned,
        total_wx * scale,
        total_wh * scale,
        total_b * scale,
        total_w * scale,
        total_wb * scale,
    )


def solution(mesh):
    return jax.shard_map(
        body,
        mesh=mesh,
        in_specs=(
            P("replica", ("outer", "link"), None),
            P("replica", ("outer", "link"), None),
            P("replica", ("outer", "link"), None),
            P("replica", ("outer", "link")),
            P("replica", ("outer", "link")),
            P("replica", None, ("outer", "link"), None),
            P("replica", ("outer", "link"), None),
            P("replica", ("outer", "link"), None),
            P(),
            P(),
            P(),
            P(),
            P(),
            P(),
            P(),
        ),
        out_specs=(
            P("replica", ("outer", "link"), None),
            P("replica", ("outer", "link"), None),
            P("replica", ("outer", "link"), None),
            P("replica", ("outer", "link"), None),
            P(),
            P(),
            P(),
            P(),
            P(),
            P(),
            P(),
        ),
        check_vma=False,
    )
```

time: 536 us -> 274 us (0.51); the launches traced: 530 us -> 274 us
  matrix products: 182 us -> 0 us
  other arithmetic: 130 us -> 4.53 us
  Pallas kernels: 0 us -> 49.7 us
  local copies, waits for them, and re-layouts: 48.9 us -> 10.8 us
  waiting for transfers between devices: 92.1 us -> 118 us
  blocking collectives: 41.4 us -> 61.8 us
    dot_general x201 -> x0, matrix products: 182 us -> none  [the longest x48 50.9 us: gate_terms(): jnp.dot(hop_input, input_weight, preferred_element_type=jnp.float32)]
    pallas_call x0 -> x5, Pallas kernels: none -> 49.7 us  [the longest x1 22 us: body(): call(functools.partial(backward_kernel, steps), grad_shapes(slots, flows,...]
    scatter-add x4 -> x0, other arithmetic: 48 us -> none  [the longest x1 17.7 us: body(): jax.ops.segment_sum(grad_inputs.reshape(hop_count * flow_count, feat_widt...]
    mul x81 -> x4, other arithmetic: 45.5 us -> 3.14 us  [the longest x1 1.3 us: finish(): total_w * scale]
    gather x4 -> x0, local copies, waits for them, and re-layouts: 33.5 us -> none  [the longest x1 12.9 us: body(): jnp.take(returned.reshape(group_size * slot_cap, feat_width), slot_ids, a...]
    psum x1, waiting for transfers between devices: 62.8 us -> 91.2 us  [finish(): lax.psum((grad_wx, grad_wh, grad_bias[0]), everywhere)]
    all_to_all x0 -> x1, blocking collectives: none -> 19.9 us  [swap_slots(): lax.all_to_all(blocks, ('outer', 'link'), split_axis=0, concat_axis=0, ti...]
    dynamic_update_slice x24 -> x0, other arithmetic: 18.6 us -> none  [gru_forward(): lax.scan(advance, path_start.astype(jnp.float32), (hop_inputs, live_mask))]
  transfers between devices with their start and end apart: 5 -> 4, of which waited for: 4 -> 3; matrix products, arithmetic and copies ran while one was open for 9% -> 2% of each run, Pallas kernels for 0% -> 1%
where the time goes in v1:
time: 274 us
  waiting for transfers between devices  118 us (43%)
  blocking collectives  61.8 us (23%)
  Pallas kernels  49.7 us (18%)
  starting transfers between devices  14.6 us (5%)
  between operations  14.2 us (5%)
  local copies, waits for them, and re-layouts  10.8 us (4%)
  other arithmetic  4.53 us (2%)
    psum x1, waiting for transfers between devices, finish(): lax.psum((grad_wx, grad_wh, grad_bias[0]), everywhere)  91.2 us
    psum x1, blocking collectives, finish(): lax.psum((grad_wx, grad_wh, grad_bias[0]), everywhere)  41.9 us
    all_to_all x3, waiting for transfers between devices, swap_slots(): lax.all_to_all(blocks, ('outer', 'link'), split_axis=0, concat_axis=0, ti...  26.8 us
    pallas_call x1, Pallas kernels, body(): call(functools.partial(backward_kernel, steps), grad_shapes(slots, flows,...  22 us
    all_to_all x1, blocking collectives, swap_slots(): lax.all_to_all(blocks, ('outer', 'link'), split_axis=0, concat_axis=0, ti...  19.9 us
    pallas_call x1, Pallas kernels, body(): call(functools.partial(forward_kernel, steps), [((hops * flows, width), b...  18.4 us
    all_to_all x3, starting transfers between devices, swap_slots(): lax.all_to_all(blocks, ('outer', 'link'), split_axis=0, concat_axis=0, ti...  14.6 us
  transfers between devices with their start and end apart: 4, of which 3 were waited for; matrix products, arithmetic and copies ran while one was open for 2% of the time, Pallas kernels for 1%

profile of v1, /device:TPU:0, one launch (start us, length us, event | category | flops | bytes accessed | tf_op | source)
XLA Modules:
  0.0 273.6 jit_solution(3856221182500444570)
XLA Ops:
  7.7 1.4 reduce.6
  9.1 1.3 reshape_squeeze.12.col_ref
  10.4 2.4 shard_map.230
  12.7 7.4 %all-to-all-start = ((bf16[16,64,256]{2,1,0:T(8,128)(2,1)}), bf16[16,64,256]{2,1,0:T(8,128)(2,1)S(1)}, u32[]{:S(2)}, u32[]{:S(2)}) async-start(bf16[16,64,256]{2,1,0:T(8,128)(2,1)} %bitcast.35), calls=%async_computation | async-start | bytes 1048576 | tf_op jit(solution)/shard_map/all_to_all | solution.py:246
  20.7 0.7 copy.30.lens_ref
  21.5 1.6 copy.29.col_ref
  23.1 12.7 %all-to-all-done = bf16[16,64,256]{2,1,0:T(8,128)(2,1)S(1)} async-done(((bf16[16,64,256]{2,1,0:T(8,128)(2,1)}), bf16[16,64,256]{2,1,0:T(8,128)(2,1)S(1)}, u32[]{:S(2)}, u32[]{:S(2)}) %all-to-all-start) | async-done | bytes 524320 | tf_op jit(solution)/shard_map/all_to_all | solution.py:246
  35.8 0.8 copy-done.2
  36.6 18.4 %shard_map.231 = (bf16[3072,256]{1,0:T(8,128)(2,1)}, bf16[3072,256]{1,0:T(8,128)(2,1)}, f32[3072,1280]{1,0:T(8,128)}, bf16[1024,256]{1,0:T(8,128)(2,1)}, bf16[128,256]{1,0:T(8,128)(2,1)}) custom-call(bf16[1024,256]{1,0:T(8,128)(2,1)} %bitcast.33, bf16[128,256]{1,0:T(8,128)(2,1)} %bitcast.46, s32[3072,1]{1,0:T(8,128)} %copy.29.col_ref, ...), custom_call_target="tpu_custom_call" | custom-call | tf_op jit(solution)/shard_map/pallas_call | solution.py:299
  55.0 3.6 %all-to-all-start.1 = ((bf16[16,64,256]{2,1,0:T(8,128)(2,1)}), bf16[16,64,256]{2,1,0:T(8,128)(2,1)S(1)}, u32[]{:S(2)}, u32[]{:S(2)}) async-start(bf16[16,64,256]{2,1,0:T(8,128)(2,1)} %bitcast.39), calls=%async_computation.1 | async-start | bytes 1048576 | tf_op jit(solution)/shard_map/all_to_all | solution.py:246
  59.4 0.9 copy.32.keep_ref
  60.2 14.0 %all-to-all-done.1 = bf16[16,64,256]{2,1,0:T(8,128)(2,1)S(1)} async-done(((bf16[16,64,256]{2,1,0:T(8,128)(2,1)}), bf16[16,64,256]{2,1,0:T(8,128)(2,1)S(1)}, u32[]{:S(2)}, u32[]{:S(2)}) %all-to-all-start.1) | async-done | bytes 524320 | tf_op jit(solution)/shard_map/all_to_all | solution.py:246
  74.3 0.8 copy-done.1
  75.1 4.5 %shard_map.232 = (bf16[512,256]{1,0:T(8,128)(2,1)}, f32[512,256]{1,0:T(8,128)}, bf16[1024,256]{1,0:T(8,128)(2,1)}, f32[768,256]{1,0:T(8,128)}, f32[2,256]{1,0:T(2,128)}) custom-call(bf16[1024,256]{1,0:T(8,128)(2,1)} %bitcast.32, s32[1,1024]{1,0:T(1,128)} %reshape_squeeze.11.row_ref, s32[1024,1]{1,0:T(8,128)} %reshape_squeeze.12.col_ref, ...), custom_call_target="tpu_custom_call" | custom-call | tf_op jit(solution)/shard_map/pallas_call | solution.py:335
  79.5 19.9 %all_to_all.20 = bf16[16,64,256]{2,1,0:T(8,128)(2,1)} all-to-all(bf16[16,64,256]{2,1,0:T(8,128)(2,1)} %bitcast.40), channel_id=1, replica_groups=mesh['replica'=2,'outer'=4,'link'=4] {'outer','link'}, dimensions={0} | all-to-all | bytes 1048576 | tf_op jit(solution)/shard_map/all_to_all | solution.py:246
  99.4 22.0 %shard_map.233 = (bf16[1024,256]{1,0:T(8,128)(2,1)}, f32[128,256]{1,0:T(8,128)}, f32[256,768]{1,0:T(8,128)}, f32[256,768]{1,0:T(8,128)}, f32[1,768]{1,0:T(1,128)}) custom-call(bf16[1024,256]{1,0:T(8,128)(2,1)} %bitcast.34, bf16[128,256]{1,0:T(8,128)(2,1)} %bitcast.45, s32[3072,1]{1,0:T(8,128)} %copy.29.col_ref, s32[6,1,512]{2,1,0:T(1,128)} %bitcast.43, ...), custom_call_target="tpu_custom_call" | custom-call | tf_op jit(solution)/shard_map/pallas_call | solution.py:360
  121.5 3.6 %all-to-all-start.3 = ((bf16[16,64,256]{2,1,0:T(8,128)(2,1)}), bf16[16,64,256]{2,1,0:T(8,128)(2,1)S(1)}, u32[]{:S(2)}, u32[]{:S(2)}) async-start(bf16[16,64,256]{2,1,0:T(8,128)(2,1)} %bitcast.22), calls=%async_computation.3 | async-start | bytes 1048576 | tf_op jit(solution)/shard_map/all_to_all | solution.py:246
  125.2 41.9 %all-reduce = (f32[768]{0:T(1024)S(1)}, f32[2,256]{1,0:T(2,128)S(1)}) all-reduce(f32[768]{0:T(1024)S(1)} %reduce.2, f32[2,256]{1,0:T(2,128)S(1)} %copy-done.9), channel_id=1, replica_groups=mesh['replica'=2,'outer'=4,'link'=4] {'replica','outer','link'}, use_global_device_ids=true, to_apply=%region_2.0 | all-reduce | flops 1280 | bytes 10240 | tf_op jit(solution)/shard_map/psum | solution.py:438
  168.2 0.8 copy-done
  169.0 2.4 shard_map.234
  171.4 91.2 %all-reduce.4.cloned.1.call-done = (f32[256,768]{1,0:T(8,128)}, f32[256,768]{1,0:T(8,128)}, f32[768,256]{1,0:T(8,128)}) async-done(((f32[256,768]{1,0:T(8,128)}, f32[256,768]{1,0:T(8,128)}, f32[768,256]{1,0:T(8,128)}), (f32[256,768]{1,0:T(8,128)}, f32[256,768]{1,0:T(8,128)}, f32[768,256]{1,0:T(8,128)})) %all-reduce.4.cloned.1.call-update) | async-done | bytes 2359312 | tf_op jit(solution)/shard_map/psum | solution.py:438
  262.6 1.3 broadcast_multiply_fusion
  264.6 0.8 slice.16
  265.5 1.2 broadcast_multiply_fusion.1
  (33 shorter events, 3.8 us)
Async XLA Ops:
  7.2 13.0 %copy-start.7 = (f32[768]{0:T(1024)S(1)}, f32[768]{0:T(1024)}, u32[]{:S(2)}) copy-start(f32[768]{0:T(1024)} %param.25) | copy-start | bytes 9220
  7.2 13.5 %copy-start.11 = (s32[1,128]{1,0:T(1,128)S(1)}, s32[1,128]{1,0:T(1,128)}, u32[]{:S(2)}) copy-start(s32[1,128]{1,0:T(1,128)} %param.18) | copy-start | bytes 1540
  7.2 14.3 %copy-start.5 = (s32[1,128,24]{1,2,0:T(8,128)S(1)}, s32[1,128,24]{1,2,0:T(8,128)}, u32[]{:S(2)}) copy-start(s32[1,128,24]{1,2,0:T(8,128)} %param.17) | copy-start | bytes 36868
  12.7 23.1 %all-to-all-start = ((bf16[16,64,256]{2,1,0:T(8,128)(2,1)}), bf16[16,64,256]{2,1,0:T(8,128)(2,1)S(1)}, u32[]{:S(2)}, u32[]{:S(2)}) async-start(bf16[16,64,256]{2,1,0:T(8,128)(2,1)} %bitcast.35), calls=%async_computation | async-start | bytes 1048576 | tf_op jit(solution)/shard_map/all_to_all | solution.py:246
  35.8 0.8 copy-start.2
  36.6 22.1 %copy-start.6 = (s32[1,16,1,64]{3,2,1,0:T(1,128)S(1)}, s32[1,16,1,64]{3,2,1,0:T(1,128)}, u32[]{:S(2)}) copy-start(s32[1,16,1,64]{3,2,1,0:T(1,128)} %param.20) | copy-start | bytes 12292
  36.6 22.7 %copy-start.10 = (s32[1,512]{1,0:T(1,128)S(1)}, s32[1,512]{1,0:T(1,128)}, u32[]{:S(2)}) copy-start(s32[1,512]{1,0:T(1,128)} %param.19) | copy-start | bytes 6148
  55.0 19.2 %all-to-all-start.1 = ((bf16[16,64,256]{2,1,0:T(8,128)(2,1)}), bf16[16,64,256]{2,1,0:T(8,128)(2,1)S(1)}, u32[]{:S(2)}, u32[]{:S(2)}) async-start(bf16[16,64,256]{2,1,0:T(8,128)(2,1)} %bitcast.39), calls=%async_computation.1 | async-start | bytes 1048576 | tf_op jit(solution)/shard_map/all_to_all | solution.py:246
  58.6 204.0 %all-reduce.4.cloned.1.call-start = ((), (), s32[]{:S(2)}) async-start(), calls=%async_computation.4 | async-start | bytes 4718592 | tf_op jit(solution)/shard_map/psum | solution.py:438
  74.3 0.8 copy-start.1
  121.5 3.6 %copy-start.8 = (f32[1,768]{1,0:T(1,128)S(1)}, f32[1,768]{1,0:T(1,128)}, u32[]{:S(2)}) copy-start(f32[1,768]{1,0:T(1,128)} %get-tuple-element.38) | copy-start | bytes 9220
  121.5 3.7 %copy-start.9 = (f32[2,256]{1,0:T(2,128)S(1)}, f32[2,256]{1,0:T(2,128)}, u32[]{:S(2)}) copy-start(f32[2,256]{1,0:T(2,128)} %get-tuple-element.40) | copy-start | bytes 6148
  121.5 46.7 %all-to-all-start.3 = ((bf16[16,64,256]{2,1,0:T(8,128)(2,1)}), bf16[16,64,256]{2,1,0:T(8,128)(2,1)S(1)}, u32[]{:S(2)}, u32[]{:S(2)}) async-start(bf16[16,64,256]{2,1,0:T(8,128)(2,1)} %bitcast.22), calls=%async_computation.3 | async-start | bytes 1048576 | tf_op jit(solution)/shard_map/all_to_all | solution.py:246
  168.2 0.8 copy-start
  262.6 2.9 %copy-start.3 = (f32[256,768]{1,0:T(8,128)S(1)}, f32[256,768]{1,0:T(8,128)}, u32[]{:S(2)}) copy-start(f32[256,768]{1,0:T(8,128)} %get-tuple-element.43) | copy-start | bytes 2359300
  262.6 2.9 %copy-start.4 = (f32[256,768]{1,0:T(8,128)S(1)}, f32[256,768]{1,0:T(8,128)}, u32[]{:S(2)}) copy-start(f32[256,768]{1,0:T(8,128)} %get-tuple-element.44) | copy-start | bytes 2359300
Sparse Core Ops, SparseCore 0:
  121.6 140.9 all-reduce.3

commit v2 on v1

--- a/solution.py
+++ b/solution.py
@@ -8,6 +8,8 @@
 from jax.sharding import PartitionSpec as P
 
 VMEM_BYTES = 56 * 1024 * 1024
+MESH = pl.DeviceIdType.MESH
+LANES = 128
 
 
 def mm(a, b):
@@ -40,9 +42,57 @@
     return pl.BlockSpec(memory_space=memory_space)
 
 
-def serve_kernel(col_ref, link_ref, out_ref):
+def group_place():
+    span = lax.axis_size("link")
+    size = lax.axis_size("outer") * span
+    return lax.axis_index("outer") * span + lax.axis_index("link"), size, span
+
+
+def greet(axes):
+    barrier = pltpu.get_barrier_semaphore()
+    me, size, span = group_place()
+    count = size - 1
+    for k in range(1, size):
+        peer = lax.rem(me + k, size)
+        where = {"outer": lax.div(peer, span), "link": lax.rem(peer, span)}
+        pl.semaphore_signal(barrier, inc=1, device_id=where, device_id_type=MESH)
+    for axis in axes:
+        n = lax.axis_size(axis)
+        count += n - 1
+        for k in range(1, n):
+            where = {axis: lax.rem(lax.axis_index(axis) + k, n)}
+            pl.semaphore_signal(barrier, inc=1, device_id=where, device_id_type=MESH)
+    return barrier, count
+
+
+def start_exchange(src, dst, send_sem, recv_sem):
+    me, size, span = group_place()
+    cap = src.shape[0] // size
+    mine = pl.ds(pl.multiple_of(me * cap, cap), cap)
+    copies = []
+    for k in range(1, size):
+        peer = lax.rem(me + k, size)
+        copy = pltpu.make_async_remote_copy(
+            src_ref=src.at[pl.ds(pl.multiple_of(peer * cap, cap), cap)],
+            dst_ref=dst.at[mine],
+            send_sem=send_sem.at[k - 1],
+            recv_sem=recv_sem.at[k - 1],
+            device_id={"outer": lax.div(peer, span), "link": lax.rem(peer, span)},
+            device_id_type=MESH,
+        )
+        copy.start()
+        copies.append(copy)
+    dst[mine, :] = src[mine, :]
+    return copies
+
+
+def serve_kernel(col_ref, link_ref, out_ref, served, send_sem, recv_sem):
+    barrier, count = greet(())
     hot = one_hot_rows(col_ref[...], link_ref.shape[0])
-    out_ref[...] = mm(hot, link_ref[...]).astype(jnp.bfloat16)
+    served[...] = mm(hot, link_ref[...]).astype(jnp.bfloat16)
+    pl.semaphore_wait(barrier, count)
+    for copy in start_exchange(served, out_ref, send_sem, recv_sem):
+        copy.wait()
 
 
 def forward_kernel(
@@ -109,7 +159,7 @@
 
 
 def link_kernel(
-    arrived_ref,
+    partial_ref,
     row_ref,
     col_ref,
     link_ref,
@@ -121,31 +171,198 @@
     b2_ref,
     link_out_ref,
     direct_ref,
-    back_ref,
+    returned_ref,
     grad_w_ref,
     grad_b_ref,
+    arrived,
+    back,
+    send_sem,
+    recv_sem,
 ):
+    barrier, count = greet(())
+    pl.semaphore_wait(barrier, count)
+    incoming = start_exchange(partial_ref, arrived, send_sem.at[0], recv_sem.at[0])
     links, width = link_ref.shape
     rows = link_ref[...]
     keep = keep_ref[...]
-    agg = mm(one_hot_cols(row_ref[...], links), arrived_ref[...]).astype(jnp.bfloat16)
-    u = mm(rows, w1_ref[:width, :]) + mm(agg, w1_ref[width:, :]) + b1_ref[...]
+    gv = keep * grad_ref[...].astype(jnp.float32)
+    gv_bf = gv.astype(jnp.bfloat16)
+    d_act = mm_nt(gv_bf, w2_ref[...])
+    u = mm(rows, w1_ref[:width, :]) + b1_ref[...]
+    for copy in incoming:
+        copy.wait()
+    agg = mm(one_hot_cols(row_ref[...], links), arrived[...]).astype(jnp.bfloat16)
+    u = u + mm(agg, w1_ref[width:, :])
     s = sigmoid(u)
+    du = d_act * s * (1.0 + u * (1.0 - s))
+    du_bf = du.astype(jnp.bfloat16)
+    d_agg = mm_nt(du_bf, w1_ref[width:, :]).astype(jnp.bfloat16)
+    back[...] = mm(one_hot_rows(col_ref[...], links), d_agg).astype(jnp.bfloat16)
+    outgoing = start_exchange(back, returned_ref, send_sem.at[1], recv_sem.at[1])
     act = (u * s).astype(jnp.bfloat16)
     value = rows.astype(jnp.float32) + mm(act, w2_ref[...]) + b2_ref[...]
     link_out_ref[...] = (keep * value).astype(jnp.bfloat16)
-    gv = keep * grad_ref[...].astype(jnp.float32)
-    gv_bf = gv.astype(jnp.bfloat16)
-    du = mm_nt(gv_bf, w2_ref[...]) * s * (1.0 + u * (1.0 - s))
-    du_bf = du.astype(jnp.bfloat16)
-    d_agg = mm_nt(du_bf, w1_ref[width:, :]).astype(jnp.bfloat16)
-    back_ref[...] = mm(one_hot_rows(col_ref[...], links), d_agg).astype(jnp.bfloat16)
     direct_ref[...] = gv + mm_nt(du_bf, w1_ref[:width, :])
-    grad_w_ref[:width, :] = mm_tn(rows, du_bf)
-    grad_w_ref[width : 2 * width, :] = mm_tn(agg, du_bf)
-    grad_w_ref[2 * width :, :] = mm_tn(act, gv_bf)
-    grad_b_ref[0:1, :] = jnp.sum(du, axis=0, keepdims=True)
-    grad_b_ref[1:2, :] = jnp.sum(gv, axis=0, keepdims=True)
+    grads = (mm_tn(rows, du_bf), mm_tn(agg, du_bf), mm_tn(act, gv_bf))
+    for k, grad in enumerate(grads):
+        put_lanes(grad_w_ref, grad, 3 * width, k * width)
+    grad_b_ref[...] = jnp.zeros_like(grad_b_ref)
+    for k, term in enumerate((du, gv)):
+        put_lanes(grad_b_ref, jnp.sum(term, axis=0, keepdims=True), 1, k * (width // LANES))
+    for copy in outgoing:
+        copy.wait()
+
+
+def put_lanes(out_ref, value, pitch, first):
+    for k in range(value.shape[1] // LANES):
+        piece = value[:, k * LANES : (k + 1) * LANES].astype(out_ref.dtype)
+        out_ref[pl.ds(k * pitch + first, value.shape[0]), :] = piece
+
+
+def get_lanes(ref, part, pitch, first, count, width):
+    pieces = [
+        ref[part, pl.ds(k * pitch + first, count), :].astype(jnp.float32)
+        for k in range(width // LANES)
+    ]
+    return jnp.concatenate(pieces, axis=1)
+
+
+ORDERS = (
+    ("outer", "replica", "link"),
+    ("replica", "outer", "link"),
+    ("replica", "outer", "link"),
+)
+
+
+def reduce_layout(rows, order):
+    places, size, offset = [], rows, 0
+    for axis in order:
+        n = lax.axis_size(axis)
+        size = size // n
+        places.append((axis, n, size, offset))
+        offset = offset + lax.axis_index(axis) * size
+    return places
+
+
+def send_all(axis, n, source, target, send_sem, recv_sem):
+    copies = []
+    for k in range(1, n):
+        peer = lax.rem(lax.axis_index(axis) + k, n)
+        copy = pltpu.make_async_remote_copy(
+            src_ref=source(peer),
+            dst_ref=target(k - 1),
+            send_sem=send_sem.at[k - 1],
+            recv_sem=recv_sem.at[k - 1],
+            device_id={axis: peer},
+            device_id_type=MESH,
+        )
+        copy.start()
+        copies.append(copy)
+    return copies
+
+
+def tail_kernel(
+    dpart_ref,
+    first_ref,
+    second_ref,
+    third_ref,
+    bias_a_ref,
+    bias_b_ref,
+    owned_ref,
+    sums_ref,
+    bias_ref,
+    *scratch,
+):
+    landing = scratch[:9]
+    held = scratch[9:15]
+    bias_now, bias_in, send_sem, recv_sem, swap_send, swap_recv = scratch[15:]
+    barrier, count = greet(("replica", "outer", "link"))
+    bias_now[0, :8, :] = bias_a_ref[...]
+    bias_now[0, 8:, :] = bias_b_ref[...]
+    pl.semaphore_wait(barrier, count)
+    inputs = (first_ref, second_ref, third_ref)
+    rows = first_ref.shape[0]
+    layouts = [reduce_layout(rows, order) for order in ORDERS]
+    swaps = []
+    for phase in range(3):
+        started = []
+        for part in range(3):
+            axis, n, size, _ = layouts[part][phase]
+            now = inputs[part] if phase == 0 else held[part * 2 + phase - 1]
+            land = landing[part * 3 + phase]
+
+            def source(peer, now=now, size=size):
+                return now.at[pl.ds(pl.multiple_of(peer * size, 16), size)]
+
+            started.append(
+                send_all(
+                    axis,
+                    n,
+                    source,
+                    lambda k, land=land: land.at[k],
+                    send_sem.at[part, phase],
+                    recv_sem.at[part, phase],
+                )
+            )
+        axis, n = layouts[0][phase][:2]
+        started.append(
+            send_all(
+                axis,
+                n,
+                lambda peer, phase=phase: bias_now.at[phase],
+                lambda k, phase=phase: bias_in.at[phase, k],
+                send_sem.at[3, phase],
+                recv_sem.at[3, phase],
+            )
+        )
+        if phase == 0:
+            swaps = start_exchange(dpart_ref, owned_ref, swap_send, swap_recv)
+        for part in range(3):
+            axis, n, size, offset = layouts[part][phase]
+            now = inputs[part] if phase == 0 else held[part * 2 + phase - 1]
+            land = landing[part * 3 + phase]
+            for copy in started[part]:
+                copy.wait()
+            place = lax.axis_index(axis)
+            mine = now[pl.ds(pl.multiple_of(place * size, 16), size), :].astype(jnp.float32)
+            for k in range(n - 1):
+                mine = mine + land[k].astype(jnp.float32)
+            mine = mine.astype(jnp.bfloat16)
+            if phase < 2:
+                held[part * 2 + phase][...] = mine
+            else:
+                sums_ref[part, pl.ds(pl.multiple_of(offset + place * size, 16), size), :] = mine
+        for copy in started[3]:
+            copy.wait()
+        total = bias_now[phase]
+        for k in range(n_of(layouts[0][phase]) - 1):
+            total = total + bias_in[phase, k]
+        if phase < 2:
+            bias_now[phase + 1] = total
+        else:
+            bias_ref[...] = total
+    for phase in (2, 1, 0):
+        started = []
+        for part in range(3):
+            axis, n, size, offset = layouts[part][phase]
+            start = pl.multiple_of(offset + lax.axis_index(axis) * size, 16)
+            region = sums_ref.at[part, pl.ds(start, size)]
+            started += send_all(
+                axis,
+                n,
+                lambda peer, region=region: region,
+                lambda k, region=region: region,
+                send_sem.at[part, 3 + phase],
+                recv_sem.at[part, 3 + phase],
+            )
+        for copy in started:
+            copy.wait()
+    for copy in swaps:
+        copy.wait()
+
+
+def n_of(place):
+    return place[1]
 
 
 def backward_kernel(
@@ -221,30 +438,91 @@
         emit_grads(acc_wx, acc_wh, acc_b, grad_wx_ref, grad_wh_ref, grad_b_ref)
 
 
-def collect_kernel(owned_ref, row_ref, direct_ref, out_ref):
+def collect_kernel(
+    scale,
+    owned_ref,
+    row_ref,
+    direct_ref,
+    sums_ref,
+    bias_ref,
+    out_ref,
+    wx_ref,
+    wh_ref,
+    bias_out_ref,
+    w1_ref,
+    b1_ref,
+    w2_ref,
+    b2_ref,
+):
+    width = direct_ref.shape[1]
     hot = one_hot_cols(row_ref[...], direct_ref.shape[0])
     out_ref[...] = direct_ref[...] + mm(hot, owned_ref[...])
-
-
-def call(kernel, out_shapes, **options):
+    wx_ref[...] = get_lanes(sums_ref, 0, width, 0, width, 3 * width) * scale
+    wh_ref[...] = get_lanes(sums_ref, 1, width, 0, width, 3 * width) * scale
+    w1_ref[...] = get_lanes(sums_ref, 2, 3 * width, 0, 2 * width, width) * scale
+    w2_ref[...] = get_lanes(sums_ref, 2, 3 * width, 2 * width, width, width) * scale
+    bias = bias_ref[...] * scale
+    for k in range(3 * width // LANES):
+        bias_out_ref[:, k * LANES : (k + 1) * LANES] = bias[k : k + 1, :]
+    for k in range(width // LANES):
+        lanes = slice(k * LANES, (k + 1) * LANES)
+        b1_ref[:, lanes] = bias[8 + k : 9 + k, :]
+        b2_ref[:, lanes] = bias[8 + width // LANES + k : 9 + width // LANES + k, :]
+
+
+def call(kernel, out_shapes, collective_id=None, **options):
     return pl.pallas_call(
         kernel,
         out_shape=[jax.ShapeDtypeStruct(shape, dtype) for shape, dtype in out_shapes],
-        compiler_params=pltpu.CompilerParams(vmem_limit_bytes=VMEM_BYTES),
+        compiler_params=pltpu.CompilerParams(
+            vmem_limit_bytes=VMEM_BYTES,
+            collective_id=collective_id,
+            has_side_effects=collective_id is not None,
+        ),
         **options,
     )
 
 
 def emit_grads(acc_wx, acc_wh, acc_b, grad_wx_ref, grad_wh_ref, grad_b_ref):
-    grad_wx_ref[...] = acc_wx[...]
-    grad_wh_ref[...] = acc_wh[...]
-    grad_b_ref[...] = jnp.sum(acc_b[...], axis=0, keepdims=True)
-
-
-def swap_slots(rows, group, cap):
-    blocks = rows.reshape(group, cap, rows.shape[1])
-    moved = lax.all_to_all(blocks, ("outer", "link"), split_axis=0, concat_axis=0, tiled=True)
-    return moved.reshape(group * cap, rows.shape[1])
+    width = acc_wx.shape[0]
+    put_lanes(grad_wx_ref, acc_wx[...], width, 0)
+    put_lanes(grad_wh_ref, acc_wh[...], width, 0)
+    grad_b_ref[...] = jnp.zeros_like(grad_b_ref)
+    put_lanes(grad_b_ref, jnp.sum(acc_b[...], axis=0, keepdims=True), 1, 0)
+
+
+def grad_shapes(slots, flows, width):
+    rows = 3 * width * width // LANES
+    return [
+        ((slots, width), jnp.bfloat16),
+        ((flows, width), jnp.float32),
+        ((rows, LANES), jnp.bfloat16),
+        ((rows, LANES), jnp.bfloat16),
+        ((8, LANES), jnp.float32),
+    ]
+
+
+def tail_scratch(rows):
+    bf, f32 = jnp.bfloat16, jnp.float32
+    landing, held = [], []
+    for order in ORDERS:
+        size = rows
+        for phase, axis in enumerate(order):
+            n = lax.axis_size(axis)
+            size = size // n
+            landing.append(pltpu.VMEM((n - 1, size, LANES), bf))
+            if phase < 2:
+                held.append(pltpu.VMEM((size, LANES), bf))
+    most = max(lax.axis_size(axis) for axis in ORDERS[0]) - 1
+    peers = lax.axis_size("outer") * lax.axis_size("link") - 1
+    return landing + held + [
+        pltpu.VMEM((3, 16, LANES), f32),
+        pltpu.VMEM((3, most, 16, LANES), f32),
+        pltpu.SemaphoreType.DMA((4, 6, most)),
+        pltpu.SemaphoreType.DMA((4, 6, most)),
+        pltpu.SemaphoreType.DMA((peers,)),
+        pltpu.SemaphoreType.DMA((peers,)),
+    ]
 
 
 def body(
@@ -282,10 +560,19 @@
     keep_col = (1 - failed[0]).astype(f32)[:, None]
     span = steps * flows
 
-    served = call(
-        serve_kernel, [((slots, width), bf)], in_specs=[whole()] * 2, out_specs=[whole()]
+    peers = group - 1
+    fetched = call(
+        serve_kernel,
+        [((slots, width), bf)],
+        collective_id=0,
+        in_specs=[whole()] * 2,
+        out_specs=[whole()],
+        scratch_shapes=[
+            pltpu.VMEM((slots, width), bf),
+            pltpu.SemaphoreType.DMA((peers,)),
+            pltpu.SemaphoreType.DMA((peers,)),
+        ],
     )(serve_col, link_rows)[0]
-    fetched = swap_slots(served, group, cap)
 
     def fixed(*shape):
         return pl.BlockSpec(shape, lambda i: (0,) * len(shape))
@@ -330,21 +617,26 @@
             pltpu.VMEM((span, width), bf),
         ],
     )(fetched, path_in[0], slot_col, slot_row, lens_col, gru_wx, gru_wh, gru_bias[None])
-    arrived = swap_slots(partial_value, group, cap)
-
-    link_out, direct, back, grad_w, grad_b = call(
+    link_out, direct, returned, grad_w, grad_b = call(
         link_kernel,
         [
             ((links, width), bf),
             ((links, width), f32),
             ((slots, width), bf),
-            ((3 * width, width), f32),
-            ((2, width), f32),
-        ],
+            ((3 * width * width // LANES, LANES), bf),
+            ((8, LANES), f32),
+        ],
+        collective_id=1,
         in_specs=[whole()] * 10,
         out_specs=[whole()] * 5,
+        scratch_shapes=[
+            pltpu.VMEM((slots, width), bf),
+            pltpu.VMEM((slots, width), bf),
+            pltpu.SemaphoreType.DMA((2, peers)),
+            pltpu.SemaphoreType.DMA((2, peers)),
+        ],
     )(
-        arrived,
+        partial_value,
         serve_row,
         serve_col,
         link_rows,
@@ -355,8 +647,6 @@
         mlp_w2,
         mlp_b2[None],
     )
-    returned = swap_slots(back, group, cap)
-
     dpart, path_back, grad_wx, grad_wh, grad_bias = call(
         functools.partial(backward_kernel, steps),
         grad_shapes(slots, flows, width),
@@ -396,15 +686,36 @@
         hs,
         coef,
     )
-    everywhere = ("replica", "outer", "link")
     devices = lax.axis_size("replica") * lax.axis_size("outer") * lax.axis_size("link")
     scale = float(devices * links) ** (-0.5)
-    owned, total_wx, total_wh, total_b, total_w, total_wb = finish(
-        dpart, grad_wx, grad_wh, grad_bias, grad_w, grad_b, group, cap, scale, everywhere
-    )
-    link_back = call(
-        collect_kernel, [((links, width), f32)], in_specs=[whole()] * 3, out_specs=[whole()]
-    )(owned, serve_row, direct)[0]
+    rows = grad_w.shape[0]
+    padded = -(-rows // (16 * devices)) * 16 * devices
+    grads = [grad_wx, grad_wh, grad_w]
+    if padded != rows:
+        grads = [jnp.pad(grad, ((0, padded - rows), (0, 0))) for grad in grads]
+    owned, sums, biases = call(
+        tail_kernel,
+        [((slots, width), bf), ((3, padded, LANES), bf), ((16, LANES), f32)],
+        collective_id=2,
+        in_specs=[whole()] * 6,
+        out_specs=[whole()] * 3,
+        scratch_shapes=tail_scratch(padded),
+    )(dpart, *grads, grad_bias, grad_b)
+    link_back, total_wx, total_wh, total_b, total_w1, total_b1, total_w2, total_b2 = call(
+        functools.partial(collect_kernel, scale),
+        [
+            ((links, width), f32),
+            ((width, 3 * width), f32),
+            ((width, 3 * width), f32),
+            ((1, 3 * width), f32),
+            ((2 * width, width), f32),
+            ((1, width), f32),
+            ((width, width), f32),
+            ((1, width), f32),
+        ],
+        in_specs=[whole()] * 5,
+        out_specs=[whole()] * 8,
+    )(owned, serve_row, direct, sums, biases)
     return (
         link_out[None],
         path_out[None],
@@ -412,37 +723,11 @@
         path_back[None],
         total_wx,
         total_wh,
-        total_b,
-        total_w[: 2 * width],
-        total_wb[0],
-        total_w[2 * width :],
-        total_wb[1],
-    )
-
-
-def grad_shapes(slots, flows, width):
-    return [
-        ((slots, width), jnp.bfloat16),
-        ((flows, width), jnp.float32),
-        ((width, 3 * width), jnp.float32),
-        ((width, 3 * width), jnp.float32),
-        ((1, 3 * width), jnp.float32),
-    ]
-
-
-def finish(
-    dpart, grad_wx, grad_wh, grad_bias, grad_w, grad_b, group, cap, scale, everywhere
-):
-    total_w, total_wb = lax.psum((grad_w, grad_b), everywhere)
-    owned = swap_slots(dpart, group, cap)
-    total_wx, total_wh, total_b = lax.psum((grad_wx, grad_wh, grad_bias[0]), everywhere)
-    return (
-        owned,
-        total_wx * scale,
-        total_wh * scale,
-        total_b * scale,
-        total_w * scale,
-        total_wb * scale,
+        total_b[0],
+        total_w1,
+        total_b1[0],
+        total_w2,
+        total_b2[0],
     )
 
 

time: 274 us -> 161 us (0.59)
  waiting for transfers between devices: 118 us -> 0 us
  Pallas kernels: 49.7 us -> 148 us
  blocking collectives: 61.8 us -> 0 us
  starting transfers between devices: 14.6 us -> 0 us
  between operations: 14.2 us -> 0.7 us
    psum x1 -> x0, waiting for transfers between devices: 91.2 us -> none  [finish(): lax.psum((grad_wx, grad_wh, grad_bias[0]), everywhere)]
    pallas_call x2 -> x3, Pallas kernels: 4.82 us -> 74 us  [the longest x1 50.1 us: body(): call(tail_kernel, [((slots, width), bf), ((3, padded, LANES), bf), ((16,...]
    psum x1 -> x0, blocking collectives: 41.9 us -> none  [finish(): lax.psum((grad_wx, grad_wh, grad_bias[0]), everywhere)]
    pallas_call x1, Pallas kernels: 4.47 us -> 33.4 us  [body(): call(link_kernel, [((links, width), bf), ((links, width), f32), ((slots,...]
    all_to_all x3 -> x0, waiting for transfers between devices: 26.8 us -> none  [swap_slots(): lax.all_to_all(blocks, ('outer', 'link'), split_axis=0, concat_axis=0, ti...]
    all_to_all x1 -> x0, blocking collectives: 19.9 us -> none  [swap_slots(): lax.all_to_all(blocks, ('outer', 'link'), split_axis=0, concat_axis=0, ti...]
    all_to_all x3 -> x0, starting transfers between devices: 14.6 us -> none  [swap_slots(): lax.all_to_all(blocks, ('outer', 'link'), split_axis=0, concat_axis=0, ti...]
    mul x4 -> x0, other arithmetic: 3.14 us -> none  [the longest x1 1.3 us: finish(): total_w * scale]
  transfers between devices with their start and end apart: 4 -> 0, of which waited for: 3 -> 0; matrix products, arithmetic and copies ran while one was open for 2% -> 0% of each run, Pallas kernels for 1% -> 0%
where the time goes in v2:
time: 161 us
  Pallas kernels  148 us (92%)
  local copies, waits for them, and re-layouts  9.02 us (6%)
  other arithmetic  3.35 us (2%)
    pallas_call x1, Pallas kernels, body(): call(tail_kernel, [((slots, width), bf), ((3, padded, LANES), bf), ((16,...  50.1 us
    pallas_call x1, Pallas kernels, body(): call(link_kernel, [((links, width), bf), ((links, width), f32), ((slots,...  33.4 us
    pallas_call x1, Pallas kernels, body(): call(functools.partial(backward_kernel, steps), grad_shapes(slots, flows,...  21.8 us
    pallas_call x1, Pallas kernels, body(): call(serve_kernel, [((slots, width), bf)], collective_id=0, in_specs=[who...  20.3 us
    pallas_call x1, Pallas kernels, body(): call(functools.partial(forward_kernel, steps), [((hops * flows, width), b...  18.4 us
    pallas_call x1, Pallas kernels, body(): call(functools.partial(collect_kernel, scale), [((links, width), f32), ((...  3.61 us

profile of v2, /device:TPU:0, one launch (start us, length us, event | category | flops | bytes accessed | tf_op | source)
XLA Modules:
  0.0 160.7 jit_solution(9318059919479524132)
XLA Ops:
  0.6 0.0 copy-start.1
  0.7 0.7 convert_bitcast_fusion
  1.3 1.3 broadcast_in_dim.22.bias_ref
  2.6 1.4 reshape_squeeze.11.row_ref
  4.0 0.5 broadcast.15
  4.5 1.4 reduce.6
  5.9 1.4 copy.30.lens_ref
  7.3 0.9 copy.32.keep_ref
  8.1 1.3 reshape_squeeze.12.col_ref
  9.4 20.3 %shard_map.230.fetched_ref = bf16[1024,256]{1,0:T(8,128)(2,1)} custom-call(s32[1024,1]{1,0:T(8,128)} %reshape_squeeze.12.col_ref, bf16[512,256]{1,0:T(8,128)(2,1)} %bitcast.23), custom_call_target="tpu_custom_call" | custom-call | tf_op jit(solution)/shard_map/pallas_call | solution.py:564
  29.7 0.0 copy-done.1
  29.7 1.7 %copy.29.col_ref = s32[3072,1]{1,0:T(8,128)} copy(s32[3072,1]{0,1:T(1,128)S(1)} %bitcast.29) | data formatting | bytes 24576 | tf_op jit(solution)/shard_map/reshape | solution.py:557
  31.4 18.4 %shard_map.231 = (bf16[3072,256]{1,0:T(8,128)(2,1)}, bf16[3072,256]{1,0:T(8,128)(2,1)}, f32[3072,1280]{1,0:T(8,128)}, bf16[1024,256]{1,0:T(8,128)(2,1)}, bf16[128,256]{1,0:T(8,128)(2,1)}) custom-call(bf16[1024,256]{1,0:T(8,128)(2,1)} %shard_map.230.fetched_ref, bf16[128,256]{1,0:T(8,128)(2,1)} %bitcast.31, s32[3072,1]{1,0:T(8,128)} %copy.29.col_ref, ...), custom_call_target="tpu_custom_call" | custom-call | tf_op jit(solution)/shard_map/pallas_call | solution.py:586
  49.8 33.4 %shard_map.232 = (bf16[512,256]{1,0:T(8,128)(2,1)}, f32[512,256]{1,0:T(8,128)}, bf16[1024,256]{1,0:T(8,128)(2,1)}, bf16[1536,128]{1,0:T(8,128)(2,1)}, f32[8,128]{1,0:T(8,128)}) custom-call(bf16[1024,256]{1,0:T(8,128)(2,1)} %get-tuple-element.37.partial_ref, s32[1,1024]{1,0:T(1,128)} %reshape_squeeze.11.row_ref, s32[1024,1]{1,0:T(8,128)} %reshape_squeeze.12.col_ref, ...), custom_call_target="tpu_custom_call" | custom-call | tf_op jit(solution)/shard_map/pallas_call | solution.py:620
  83.2 21.8 %shard_map.233 = (bf16[1024,256]{1,0:T(8,128)(2,1)}, f32[128,256]{1,0:T(8,128)}, bf16[1536,128]{1,0:T(8,128)(2,1)}, bf16[1536,128]{1,0:T(8,128)(2,1)}, f32[8,128]{1,0:T(8,128)}) custom-call(bf16[1024,256]{1,0:T(8,128)(2,1)} %get-tuple-element.40.returned_ref, bf16[128,256]{1,0:T(8,128)(2,1)} %bitcast.30, s32[3072,1]{1,0:T(8,128)} %copy.29.col_ref, ...), custom_call_target="tpu_custom_call" | custom-call | tf_op jit(solution)/shard_map/pallas_call | solution.py:650
  104.9 0.0 copy-start
  104.9 50.1 %shard_map.234 = (bf16[1024,256]{1,0:T(8,128)(2,1)}, bf16[3,1536,128]{2,1,0:T(8,128)(2,1)}, f32[16,128]{1,0:T(8,128)}) custom-call(bf16[1024,256]{1,0:T(8,128)(2,1)} %get-tuple-element.44.dpart_ref, bf16[1536,128]{1,0:T(8,128)(2,1)} %get-tuple-element.45.first_ref, bf16[1536,128]{1,0:T(8,128)(2,1)} %get-tuple-element.46.second_ref, ...), custom_call_target="tpu_custom_call" | custom-call | tf_op jit(solution)/shard_map/pallas_call | solution.py:696
  155.1 3.6 %shard_map.235 = (f32[512,256]{1,0:T(8,128)}, f32[256,768]{1,0:T(8,128)}, f32[256,768]{1,0:T(8,128)}, f32[1,768]{1,0:T(1,128)}, f32[512,256]{1,0:T(8,128)}, /*in...) custom-call(bf16[1024,256]{1,0:T(8,128)(2,1)} %get-tuple-element.50.owned_ref, ...), custom_call_target="tpu_custom_call" | custom-call | tf_op jit(solution)/shard_map/pallas_call | solution.py:704
  158.7 1.3 reduce.2
  160.0 0.0 copy-done
  160.0 0.7 copy.36
Async XLA Ops:
  0.6 29.1 %copy-start.1 = (s32[1,128,24]{1,2,0:T(8,128)S(1)}, s32[1,128,24]{1,2,0:T(8,128)}, u32[]{:S(2)}) copy-start(s32[1,128,24]{1,2,0:T(8,128)} %param.17) | copy-start | bytes 36868
  104.9 55.0 %copy-start = (bf16[512,256]{1,0:T(8,128)(2,1)S(1)}, bf16[512,256]{1,0:T(8,128)(2,1)}, u32[]{:S(2)}) copy-start(bf16[512,256]{1,0:T(8,128)(2,1)} %get-tuple-element.38) | copy-start | bytes 786436

commit v3 on v2

--- a/solution.py
+++ b/solution.py
@@ -283,80 +283,80 @@
     inputs = (first_ref, second_ref, third_ref)
     rows = first_ref.shape[0]
     layouts = [reduce_layout(rows, order) for order in ORDERS]
-    swaps = []
-    for phase in range(3):
-        started = []
+
+    def begin(part, stage):
+        if stage < 3:
+            axis, n, size, _ = layouts[part][stage]
+            now = inputs[part] if stage == 0 else held[part * 2 + stage - 1]
+            land = landing[part * 3 + stage]
+
+            def source(peer):
+                return now.at[pl.ds(pl.multiple_of(peer * size, 16), size)]
+
+            def target(k):
+                return land.at[k]
+
+        else:
+            axis, n, size, offset = layouts[part][5 - stage]
+            start = pl.multiple_of(offset + lax.axis_index(axis) * size, 16)
+
+            def source(peer):
+                return sums_ref.at[part, pl.ds(start, size)]
+
+            def target(k):
+                return sums_ref.at[part, pl.ds(start, size)]
+
+        return send_all(
+            axis, n, source, target, send_sem.at[part, stage], recv_sem.at[part, stage]
+        )
+
+    def begin_bias(phase):
+        axis, n = layouts[0][phase][:2]
+        return send_all(
+            axis,
+            n,
+            lambda peer: bias_now.at[phase],
+            lambda k: bias_in.at[phase, k],
+            send_sem.at[3, phase],
+            recv_sem.at[3, phase],
+        )
+
+    def add_up(part, phase):
+        axis, n, size, offset = layouts[part][phase]
+        now = inputs[part] if phase == 0 else held[part * 2 + phase - 1]
+        land = landing[part * 3 + phase]
+        place = lax.axis_index(axis)
+        mine = now[pl.ds(pl.multiple_of(place * size, 16), size), :].astype(jnp.float32)
+        for k in range(n - 1):
+            mine = mine + land[k].astype(jnp.float32)
+        mine = mine.astype(jnp.bfloat16)
+        if phase < 2:
+            held[part * 2 + phase][...] = mine
+        else:
+            sums_ref[part, pl.ds(pl.multiple_of(offset + place * size, 16), size), :] = mine
+
+    started = [begin(part, 0) for part in range(3)]
+    bias_copies = begin_bias(0)
+    swaps = start_exchange(dpart_ref, owned_ref, swap_send, swap_recv)
+    for stage in range(6):
         for part in range(3):
-            axis, n, size, _ = layouts[part][phase]
-            now = inputs[part] if phase == 0 else held[part * 2 + phase - 1]
-            land = landing[part * 3 + phase]
-
-            def source(peer, now=now, size=size):
-                return now.at[pl.ds(pl.multiple_of(peer * size, 16), size)]
-
-            started.append(
-                send_all(
-                    axis,
-                    n,
-                    source,
-                    lambda k, land=land: land.at[k],
-                    send_sem.at[part, phase],
-                    recv_sem.at[part, phase],
-                )
-            )
-        axis, n = layouts[0][phase][:2]
-        started.append(
-            send_all(
-                axis,
-                n,
-                lambda peer, phase=phase: bias_now.at[phase],
-                lambda k, phase=phase: bias_in.at[phase, k],
-                send_sem.at[3, phase],
-                recv_sem.at[3, phase],
-            )
-        )
-        if phase == 0:
-            swaps = start_exchange(dpart_ref, owned_ref, swap_send, swap_recv)
-        for part in range(3):
-            axis, n, size, offset = layouts[part][phase]
-            now = inputs[part] if phase == 0 else held[part * 2 + phase - 1]
-            land = landing[part * 3 + phase]
             for copy in started[part]:
                 copy.wait()
-            place = lax.axis_index(axis)
-            mine = now[pl.ds(pl.multiple_of(place * size, 16), size), :].astype(jnp.float32)
-            for k in range(n - 1):
-                mine = mine + land[k].astype(jnp.float32)
-            mine = mine.astype(jnp.bfloat16)
-            if phase < 2:
-                held[part * 2 + phase][...] = mine
+            if stage < 3:
+                add_up(part, stage)
+            if stage < 5:
+                started[part] = begin(part, stage + 1)
+        if stage < 3:
+            for copy in bias_copies:
+                copy.wait()
+            total = bias_now[stage]
+            for k in range(n_of(layouts[0][stage]) - 1):
+                total = total + bias_in[stage, k]
+            if stage < 2:
+                bias_now[stage + 1] = total
+                bias_copies = begin_bias(stage + 1)
             else:
-                sums_ref[part, pl.ds(pl.multiple_of(offset + place * size, 16), size), :] = mine
-        for copy in started[3]:
-            copy.wait()
-        total = bias_now[phase]
-        for k in range(n_of(layouts[0][phase]) - 1):
-            total = total + bias_in[phase, k]
-        if phase < 2:
-            bias_now[phase + 1] = total
-        else:
-            bias_ref[...] = total
-    for phase in (2, 1, 0):
-        started = []
-        for part in range(3):
-            axis, n, size, offset = layouts[part][phase]
-            start = pl.multiple_of(offset + lax.axis_index(axis) * size, 16)
-            region = sums_ref.at[part, pl.ds(start, size)]
-            started += send_all(
-                axis,
-                n,
-                lambda peer, region=region: region,
-                lambda k, region=region: region,
-                send_sem.at[part, 3 + phase],
-                recv_sem.at[part, 3 + phase],
-            )
-        for copy in started:
-            copy.wait()
+                bias_ref[...] = total
     for copy in swaps:
         copy.wait()
 

time: 161 us -> 154 us (0.957)
  Pallas kernels: 148 us -> 140 us
    pallas_call x1, Pallas kernels: 50.1 us -> 42.9 us  [body(): call(tail_kernel, [((slots, width), bf), ((3, padded, LANES), bf), ((16,...]
where the time goes in v3:
time: 154 us; the launch traced here: 153 us
  Pallas kernels  140 us (91%)
  local copies, waits for them, and re-layouts  9.02 us (6%)
  other arithmetic  3.35 us (2%)
    pallas_call x1, Pallas kernels, body(): call(tail_kernel, [((slots, width), bf), ((3, padded, LANES), bf), ((16,...  42.9 us
    pallas_call x1, Pallas kernels, body(): call(link_kernel, [((links, width), bf), ((links, width), f32), ((slots,...  33.4 us
    pallas_call x1, Pallas kernels, body(): call(functools.partial(backward_kernel, steps), grad_shapes(slots, flows,...  21.8 us
    pallas_call x1, Pallas kernels, body(): call(serve_kernel, [((slots, width), bf)], collective_id=0, in_specs=[who...  20.3 us
    pallas_call x1, Pallas kernels, body(): call(functools.partial(forward_kernel, steps), [((hops * flows, width), b...  18.4 us
    pallas_call x1, Pallas kernels, body(): call(functools.partial(collect_kernel, scale), [((links, width), f32), ((...  3.62 us

profile of v3, /device:TPU:0, one launch (start us, length us, event | category | flops | bytes accessed | tf_op | source)
XLA Modules:
  0.0 153.4 jit_solution(4498164864637690842)
XLA Ops:
  0.6 0.0 copy-start.1
  0.7 0.7 convert_bitcast_fusion
  1.3 1.3 broadcast_in_dim.22.bias_ref
  2.6 1.4 reshape_squeeze.11.row_ref
  4.0 0.5 broadcast.15
  4.5 1.4 reduce.6
  5.9 1.4 copy.30.lens_ref
  7.3 0.9 copy.32.keep_ref
  8.1 1.3 reshape_squeeze.12.col_ref
  9.4 20.3 %shard_map.230.fetched_ref = bf16[1024,256]{1,0:T(8,128)(2,1)} custom-call(s32[1024,1]{1,0:T(8,128)} %reshape_squeeze.12.col_ref, bf16[512,256]{1,0:T(8,128)(2,1)} %bitcast.23), custom_call_target="tpu_custom_call" | custom-call | tf_op jit(solution)/shard_map/pallas_call | solution.py:564
  29.7 0.0 copy-done.1
  29.7 1.7 %copy.29.col_ref = s32[3072,1]{1,0:T(8,128)} copy(s32[3072,1]{0,1:T(1,128)S(1)} %bitcast.29) | data formatting | bytes 24576 | tf_op jit(solution)/shard_map/reshape | solution.py:557
  31.4 18.4 %shard_map.231 = (bf16[3072,256]{1,0:T(8,128)(2,1)}, bf16[3072,256]{1,0:T(8,128)(2,1)}, f32[3072,1280]{1,0:T(8,128)}, bf16[1024,256]{1,0:T(8,128)(2,1)}, bf16[128,256]{1,0:T(8,128)(2,1)}) custom-call(bf16[1024,256]{1,0:T(8,128)(2,1)} %shard_map.230.fetched_ref, bf16[128,256]{1,0:T(8,128)(2,1)} %bitcast.31, s32[3072,1]{1,0:T(8,128)} %copy.29.col_ref, ...), custom_call_target="tpu_custom_call" | custom-call | tf_op jit(solution)/shard_map/pallas_call | solution.py:586
  49.8 33.4 %shard_map.232 = (bf16[512,256]{1,0:T(8,128)(2,1)}, f32[512,256]{1,0:T(8,128)}, bf16[1024,256]{1,0:T(8,128)(2,1)}, bf16[1536,128]{1,0:T(8,128)(2,1)}, f32[8,128]{1,0:T(8,128)}) custom-call(bf16[1024,256]{1,0:T(8,128)(2,1)} %get-tuple-element.37.partial_ref, s32[1,1024]{1,0:T(1,128)} %reshape_squeeze.11.row_ref, s32[1024,1]{1,0:T(8,128)} %reshape_squeeze.12.col_ref, ...), custom_call_target="tpu_custom_call" | custom-call | tf_op jit(solution)/shard_map/pallas_call | solution.py:620
  83.2 21.8 %shard_map.233 = (bf16[1024,256]{1,0:T(8,128)(2,1)}, f32[128,256]{1,0:T(8,128)}, bf16[1536,128]{1,0:T(8,128)(2,1)}, bf16[1536,128]{1,0:T(8,128)(2,1)}, f32[8,128]{1,0:T(8,128)}) custom-call(bf16[1024,256]{1,0:T(8,128)(2,1)} %get-tuple-element.40.returned_ref, bf16[128,256]{1,0:T(8,128)(2,1)} %bitcast.30, s32[3072,1]{1,0:T(8,128)} %copy.29.col_ref, ...), custom_call_target="tpu_custom_call" | custom-call | tf_op jit(solution)/shard_map/pallas_call | solution.py:650
  104.9 0.0 copy-start
  104.9 42.9 %shard_map.234 = (bf16[1024,256]{1,0:T(8,128)(2,1)}, bf16[3,1536,128]{2,1,0:T(8,128)(2,1)}, f32[16,128]{1,0:T(8,128)}) custom-call(bf16[1024,256]{1,0:T(8,128)(2,1)} %get-tuple-element.44.dpart_ref, bf16[1536,128]{1,0:T(8,128)(2,1)} %get-tuple-element.45.first_ref, bf16[1536,128]{1,0:T(8,128)(2,1)} %get-tuple-element.46.second_ref, ...), custom_call_target="tpu_custom_call" | custom-call | tf_op jit(solution)/shard_map/pallas_call | solution.py:696
  147.8 3.6 %shard_map.235 = (f32[512,256]{1,0:T(8,128)}, f32[256,768]{1,0:T(8,128)}, f32[256,768]{1,0:T(8,128)}, f32[1,768]{1,0:T(1,128)}, f32[512,256]{1,0:T(8,128)}, /*in...) custom-call(bf16[1024,256]{1,0:T(8,128)(2,1)} %get-tuple-element.50.owned_ref, ...), custom_call_target="tpu_custom_call" | custom-call | tf_op jit(solution)/shard_map/pallas_call | solution.py:704
  151.4 1.3 reduce.2
  152.7 0.0 copy-done
  152.7 0.7 copy.36
Async XLA Ops:
  0.6 29.1 %copy-start.1 = (s32[1,128,24]{1,2,0:T(8,128)S(1)}, s32[1,128,24]{1,2,0:T(8,128)}, u32[]{:S(2)}) copy-start(s32[1,128,24]{1,2,0:T(8,128)} %param.17) | copy-start | bytes 36868
  104.9 47.8 %copy-start = (bf16[512,256]{1,0:T(8,128)(2,1)S(1)}, bf16[512,256]{1,0:T(8,128)(2,1)}, u32[]{:S(2)}) copy-start(bf16[512,256]{1,0:T(8,128)(2,1)} %get-tuple-element.38) | copy-start | bytes 786436
